TPU v7x, 32 devices: a whole 2x2x4 slice. The times are simulated.
32 devices in a mesh: gx: 16 (over z, y, x), gy: 2 (over core).
Axes of the slice: x: 2, y: 2, z: 4, core: 2. Of those that a mesh axis runs over, the one named last changes fastest.
Arguments:
- records: float32 [98304, 128], P('gx', 'gy'), may hold values from -1.8 to 1.8
- idents: float32 [65536, 128], P('gx', 'gy'), may hold values from -1.8 to 1.8
- rec_count: int32 [98304], P('gx'), may hold values from 1 to 1000
- id_count: int32 [65536], P('gx'), may hold values from 1 to 1000
- observed: bfloat16 [3072, 128, 128], P('gx'), may hold values from -6 to 6
- send_list: int32 [256, 1], P('gx'), may hold values from 0 to 47
- slot_of_block: int32 [3072], P('gx'), may hold values from 0 to 15, as said below
- id_of_block: int32 [3072], P('gx'), may hold values from 0 to 31
Outputs:
- new_records: float32 [98304, 128], P('gx', 'gy')
- new_idents: float32 [65536, 128], P('gx', 'gy')
Inputs may be any that keep to these rules, and one draw needn't show every extreme that they name: `slot_of_block`: each owner's 192 entries use every slot from 0 to 15.
All inputs are finite; a program needn't handle non-finite values.
Results may differ from a plain program's by a relative error of at most 0.013.
Values may be sent and summed in bfloat16 or wider, within the bound.
A program may use at most 128 MiB of HBM per device.

v0:
```python
import jax
import jax.numpy as jnp
from jax import lax
from jax.sharding import PartitionSpec as P


def residual_of(summed, row_weight, col_weight, block_obs):
    weight_grid = row_weight[:, :, None] * col_weight[:, None, :]
    return (weight_grid * (summed - block_obs.astype(jnp.float32))).astype(jnp.bfloat16)


def body(records, idents, rec_count, id_count, observed, send_list, slot_of_block, id_of_block):
    peers = lax.axis_size("gx")
    blk_rows = observed.shape[1]
    half_cols = records.shape[1]
    slot_count = send_list.shape[1]
    received = peers * slot_count
    log_top = jnp.log(jnp.float32(1001.0))
    rec_bf = records.astype(jnp.bfloat16).reshape(-1, blk_rows, half_cols)
    id_bf = idents.astype(jnp.bfloat16).reshape(-1, blk_rows, half_cols)
    rec_weight = (
        (jnp.log1p(rec_count.astype(jnp.float32)) / log_top)
        .astype(jnp.bfloat16)
        .reshape(-1, blk_rows)
    )
    id_weight = (jnp.log1p(id_count.astype(jnp.float32)) / log_top).reshape(-1, blk_rows)
    sent_rows = rec_bf[send_list].reshape(peers, slot_count, blk_rows * half_cols)
    sent_weight = rec_weight[send_list]
    arrived, arrived_weight = (
        lax.all_to_all(sent_rows, "gx", split_axis=0, concat_axis=0, tiled=True),
        lax.all_to_all(sent_weight, "gx", split_axis=0, concat_axis=0, tiled=True),
    )
    left_all = arrived.reshape(received, blk_rows, half_cols)
    weight_all = arrived_weight.reshape(received, blk_rows).astype(jnp.float32)
    left_rows = left_all[slot_of_block]
    right_rows = id_bf[id_of_block]
    partial_value = jnp.einsum(
        "bik,bjk->bij", left_rows, right_rows, preferred_element_type=jnp.float32
    ).astype(jnp.bfloat16)
    summed = lax.psum(partial_value, "gy").astype(jnp.float32)
    resid = residual_of(summed, weight_all[slot_of_block], id_weight[id_of_block], observed)
    grad_left = jnp.einsum("bij,bjk->bik", resid, right_rows, preferred_element_type=jnp.float32)
    grad_right = jnp.einsum("bij,bik->bjk", resid, left_rows, preferred_element_type=jnp.float32)
    slot_grad = (
        jnp.zeros((received, blk_rows, half_cols), jnp.float32).at[slot_of_block].add(grad_left)
    )
    id_grad = jnp.zeros(id_bf.shape, jnp.float32).at[id_of_block].add(grad_right)
    returned = lax.all_to_all(
        slot_grad.reshape(peers, slot_count, blk_rows * half_cols).astype(jnp.bfloat16),
        "gx",
        split_axis=0,
        concat_axis=0,
        tiled=True,
    ).astype(jnp.float32)
    rec_grad = jnp.zeros((rec_bf.shape[0], blk_rows * half_cols), jnp.float32)
    rec_grad = rec_grad.at[send_list.reshape(-1)].add(
        returned.reshape(received, blk_rows * half_cols)
    )
    new_records = records - 0.05 * (rec_grad.reshape(records.shape) + 0.1 * records)
    new_idents = idents - 0.05 * (id_grad.reshape(idents.shape) + 0.1 * idents)
    return (new_records, new_idents)


def solution(mesh):
    in_specs = (
        P("gx", "gy"),
        P("gx", "gy"),
        P("gx"),
        P("gx"),
        P("gx", None, None),
        P("gx", None),
        P("gx"),
        P("gx"),
    )
    out_specs = (P("gx", "gy"), P("gx", "gy"))
    return jax.shard_map(body, mesh=mesh, in_specs=in_specs, out_specs=out_specs, check_vma=False)
```

profile of v0, /device:TPU:0, one launch (start us, length us, event | category | flops | bytes accessed | tf_op | source)
XLA Modules:
  0.0 179.2 jit_solution(16068006173801756498)
XLA Ops:
  7.2 0.0 copy-start.4
  7.2 0.0 copy-start.8
  7.2 0.7 fusion.9
  7.9 1.6 copy_bitcast_fusion
  9.5 0.6 gather_fusion.3
  10.2 0.3 copy.29
  10.4 0.3 reshape.148
  10.8 0.6 broadcast.53
  11.4 2.2 %reduce.1 = bf16[16,8192]{1,0:T(8,128)(2,1)S(1)} reduce(bf16[16,1,8192]{2,1,0:T(2,128)(2,1)S(1)} %reshape.148, bf16[]{:T(256)} %broadcast.53), dimensions={1}, to_apply=%reshape.148.reduce_sub_computation | reduce | bytes 524290 | tf_op jit(solution)/shard_map/reshape | solution.py:27
  13.5 0.9 reshape.152
  14.4 8.3 %all-to-all-start.1 = ((bf16[16,2,4096]{2,1,0:T(2,128)(2,1)}), bf16[16,2,4096]{2,1,0:T(2,128)(2,1)S(1)}, u32[]{:S(2)}, u32[]{:S(2)}) async-start(bf16[16,2,4096]{2,1,0:T(2,128)(2,1)} %reshape.152), calls=%async_computation.1 | async-start | bytes 524288 | tf_op jit(solution)/shard_map/all_to_all | solution.py:30
  22.8 0.0 all-reduce.2.cloned.1.call-start
  22.8 0.0 copy-done.4
  22.8 0.1 copy_bitcast_fusion.1
  22.9 0.0 copy-done.8
  23.0 0.0 copy-start.9
  23.0 2.7 %gather_fusion.5 = bf16[192,128,64]{1,2,0:T(8,128)(2,1)} fusion(bf16[32,128,64]{1,2,0:T(8,128)(2,1)S(1)} %copy_bitcast_fusion.1, s32[1024]{0:T(1024)S(1)} %pad_clamp_fusion), kind=kCustom, calls=%fused_computation.5 | custom fusion | bytes 6292224 | tf_op jit(solution)/shard_map/gather | solution.py:36
  25.7 0.0 copy-done.9
  25.8 6.9 %all-to-all-done.1 = bf16[16,2,4096]{2,1,0:T(2,128)(2,1)S(1)} async-done(((bf16[16,2,4096]{2,1,0:T(2,128)(2,1)}), bf16[16,2,4096]{2,1,0:T(2,128)(2,1)S(1)}, u32[]{:S(2)}, u32[]{:S(2)}) %all-to-all-start.1) | async-done | bytes 262176 | tf_op jit(solution)/shard_map/all_to_all | solution.py:30
  32.6 0.3 reshape.153
  32.9 1.5 reduce
  34.4 0.5 reshape.58
  35.0 0.2 copy.31
  35.2 1.2 gather_fusion.4
  36.4 0.0 copy-start
  36.4 7.6 %convolution_convert_fusion = bf16[192,128,128]{2,1,0:T(8,128)(2,1)} fusion(bf16[192,128,64]{1,2,0:T(8,128)(2,1)S(1)} %gather_fusion.4, bf16[192,128,64]{1,2,0:T(8,128)(2,1)} %gather_fusion.5), kind=kOutput, calls=%fused_computation.10 | convolution fusion | flops 405798912 | bytes 12582912 | tf_op jit(solution)/shard_map/bik,bjk->bij/dot_general | solution.py:37
  44.0 0.0 copy-done
  44.0 0.0 copy-start.6
  44.0 0.0 copy-start.7
  44.0 0.0 all-reduce.2.cloned.1.call-update
  44.0 0.7 copy-done.6
  44.7 0.6 gather_fusion
  45.3 0.6 copy.26
  45.9 3.7 %all-to-all-start = ((bf16[16,1,128]{2,1,0:T(2,128)(2,1)}), bf16[16,1,128]{2,1,0:T(2,128)(2,1)S(1)}, u32[]{:S(2)}, u32[]{:S(2)}) async-start(bf16[16,1,128]{2,1,0:T(2,128)(2,1)} %copy.26), calls=%async_computation | async-start | bytes 16384 | tf_op jit(solution)/shard_map/all_to_all | solution.py:31
  49.6 0.0 copy-done.7
  49.6 3.6 %copy.36 = f32[6144,64]{1,0:T(8,128)} copy(f32[6144,64]{0,1:T(8,128)} %param.8) | data formatting | bytes 3145728 | tf_op args[0]
  53.2 0.7 gather_fusion.2
  53.9 2.7 %all-to-all-done = bf16[16,1,128]{2,1,0:T(2,128)(2,1)S(1)} async-done(((bf16[16,1,128]{2,1,0:T(2,128)(2,1)}), bf16[16,1,128]{2,1,0:T(2,128)(2,1)S(1)}, u32[]{:S(2)}, u32[]{:S(2)}) %all-to-all-start) | async-done | bytes 4128 | tf_op jit(solution)/shard_map/all_to_all | solution.py:31
  56.6 0.7 gather_fusion.1
  57.3 16.8 %all-reduce.2.cloned.1.call-done = bf16[192,128,128]{2,1,0:T(8,128)(2,1)} async-done(((bf16[192,128,128]{2,1,0:T(8,128)(2,1)}), bf16[192,128,128]{2,1,0:T(8,128)(2,1)}) %all-reduce.2.cloned.1.call-update) | async-done | bytes 6291472 | tf_op jit(solution)/shard_map/psum | solution.py:40
  74.1 0.0 copy-done.2
  74.1 9.8 %fusion.3 = f32[192,128,64]{1,2,0:T(8,128)} fusion(bf16[192,128,64]{1,2,0:T(8,128)(2,1)S(1)} %copy-done.2, bf16[192,128,128]{2,1,0:T(8,128)(2,1)} %param.12, bf16[192,128,128]{2,1,0:T(8,128)(2,1)} %all-reduce.2.cloned.1.call-done, f32[192,128]{1,0:T(8,128)S(1)} %gather_fusion.2, f32[192,128]{1,0:T(8,128)S(1)} %gather_fusion.1), kind=kOutput, calls=%fused_computation.16 | convolution fusion | flops 421527552 | bytes 22216704 | tf_op jit(solution)/shard_map/bij,bjk->bik/dot_general | solution.py:42
  84.0 20.0 %scatter_fusion = f32[16,128,64]{1,2,0:T(8,128)S(1)} fusion(f32[16,128,64]{1,2,0:T(8,128)S(1)} %broadcast_in_dim.13, s32[192]{0:T(256)S(1)} %compare_select_fusion.1, f32[192,128,64]{1,2,0:T(8,128)} %fusion.3), kind=kCustom, calls=%fused_computation.6 | custom fusion | flops 1572864 | bytes 18875136 | tf_op jit(solution)/shard_map/scatter-add | solution.py:45
  104.0 0.7 convert_element_type.59
  104.8 2.1 %copy.33 = bf16[16,128,64]{2,1,0:T(8,128)(2,1)} copy(bf16[16,128,64]{1,2,0:T(8,128)(2,1)} %convert_element_type.59) | data formatting | bytes 524288 | tf_op jit(solution)/shard_map/convert_element_type | solution.py:49
  106.9 3.0 %convert_element_type.62 = bf16[16,1,8192]{2,1,0:T(2,128)(2,1)} reshape(bf16[16,128,64]{2,1,0:T(8,128)(2,1)} %copy.33) | data formatting | bytes 524288 | tf_op jit(solution)/shard_map/convert_element_type | solution.py:49
  109.9 3.9 %reduce.2 = bf16[16,8192]{1,0:T(8,128)(2,1)} reduce(bf16[16,1,8192]{2,1,0:T(2,128)(2,1)} %convert_element_type.62, bf16[]{:T(256)} %broadcast.53), dimensions={1}, to_apply=%convert_element_type.62.reduce_sub_computation | reduce | bytes 524290 | tf_op jit(solution)/shard_map/convert_element_type | solution.py:49
  113.8 1.8 %reshape.154 = bf16[16,2,4096]{2,1,0:T(2,128)(2,1)} reshape(bf16[16,8192]{1,0:T(8,128)(2,1)} %reduce.2) | data formatting | bytes 524288
  115.6 6.8 %all-to-all-start.2 = ((bf16[16,2,4096]{2,1,0:T(2,128)(2,1)}), bf16[16,2,4096]{2,1,0:T(2,128)(2,1)}, u32[]{:S(2)}, u32[]{:S(2)}) async-start(bf16[16,2,4096]{2,1,0:T(2,128)(2,1)} %reshape.154), calls=%async_computation.2 | async-start | bytes 524288 | tf_op jit(solution)/shard_map/all_to_all | solution.py:48
  122.4 0.0 copy-done.1
  122.5 9.3 %fusion.2 = f32[192,128,64]{1,2,0:T(8,128)} fusion(bf16[192,128,64]{1,2,0:T(8,128)(2,1)S(1)} %copy-done.1, bf16[192,128,128]{2,1,0:T(8,128)(2,1)} %param.12, bf16[192,128,128]{2,1,0:T(8,128)(2,1)} %all-reduce.2.cloned.1.call-done, f32[192,128]{1,0:T(8,128)S(1)} %gather_fusion.2, f32[192,128]{1,0:T(8,128)S(1)} %gather_fusion.1), kind=kOutput, calls=%fused_computation.15 | convolution fusion | flops 421527552 | bytes 22216704 | tf_op jit(solution)/shard_map/bij,bik->bjk/dot_general | solution.py:43
  131.8 0.1 broadcast_in_dim.31
  131.9 0.0 copy-start.5
  131.9 20.0 %scatter_fusion.1 = f32[32,128,64]{1,2,0:T(8,128)S(1)} fusion(f32[32,128,64]{1,2,0:T(8,128)S(1)} %broadcast_in_dim.31, s32[192]{0:T(256)S(1)} %compare_select_fusion, f32[192,128,64]{1,2,0:T(8,128)} %fusion.2), kind=kCustom, calls=%fused_computation.8 | custom fusion | flops 1572864 | bytes 18875136 | tf_op jit(solution)/shard_map/scatter-add | solution.py:47
  151.9 0.0 copy-done.5
  151.9 1.1 fusion.1
  153.0 0.0 all-to-all-done.2
  153.0 3.0 %reshape.155 = bf16[16,1,8192]{2,1,0:T(2,128)(2,1)} reshape(bf16[16,2,4096]{2,1,0:T(2,128)(2,1)} %all-to-all-done.2) | data formatting | bytes 524288
  156.0 2.4 %reshape.65 = f32[16,1,8192]{2,1,0:T(1,128)} convert(bf16[16,1,8192]{2,1,0:T(2,128)(2,1)} %reshape.155) | non-fusion elementwise | flops 131072 | bytes 786432 | tf_op jit(solution)/shard_map/reshape | solution.py:57
  158.4 3.2 %scatter_custom_fusion.1 = f32[48,8192]{1,0:T(8,128)} fusion(s32[16]{0:T(128)S(1)} %fusion.9, f32[]{:T(128)} %constant.8.clone.1, f32[16,1,8192]{2,1,0:T(1,128)} %reshape.65), kind=kCustom, calls=%fused_computation.19 | custom fusion | flops 131072 | bytes 2097156 | tf_op jit(solution)/shard_map/scatter-add | solution.py:56
  161.6 3.5 %reshape.62 = f32[6144,64]{1,0:T(8,128)} reshape(f32[48,8192]{1,0:T(8,128)} %scatter_custom_fusion.1) | data formatting | bytes 3145728 | tf_op jit(solution)/shard_map/reshape | solution.py:59
  165.1 0.0 copy-done.3
  165.1 4.0 %multiply_subtract_fusion = f32[6144,64]{1,0:T(8,128)} fusion(f32[6144,64]{1,0:T(8,128)S(1)} %copy-done.3, f32[6144,64]{1,0:T(8,128)} %reshape.62), kind=kLoop, calls=%fused_computation.11 | loop fusion | flops 1572864 | bytes 4718592 | tf_op jit(solution)/shard_map/sub | solution.py:59
  169.2 3.2 %copy.38 = f32[6144,64]{0,1:T(8,128)} copy(f32[6144,64]{1,0:T(8,128)} %multiply_subtract_fusion) | data formatting | bytes 3145728
  (12 shorter events, 0.1 us)
Async XLA Ops:
  7.2 15.6 %copy-start.4 = (f32[4096,64]{0,1:T(8,128)S(1)}, f32[4096,64]{0,1:T(8,128)}, u32[]{:S(2)}) copy-start(f32[4096,64]{0,1:T(8,128)} %param.9) | copy-start | bytes 3145732
  7.2 15.8 %copy-start.8 = (s32[192]{0:T(256)S(1)}, s32[192]{0:T(256)}, u32[]{:S(2)}) copy-start(s32[192]{0:T(256)} %param.15) | copy-start | bytes 2308
  14.4 18.2 %all-to-all-start.1 = ((bf16[16,2,4096]{2,1,0:T(2,128)(2,1)}), bf16[16,2,4096]{2,1,0:T(2,128)(2,1)S(1)}, u32[]{:S(2)}, u32[]{:S(2)}) async-start(bf16[16,2,4096]{2,1,0:T(2,128)(2,1)} %reshape.152), calls=%async_computation.1 | async-start | bytes 524288 | tf_op jit(solution)/shard_map/all_to_all | solution.py:30
  22.8 51.4 %all-reduce.2.cloned.1.call-start = ((), (), s32[]{:S(2)}) async-start(), calls=%async_computation.3 | async-start | bytes 12582912 | tf_op jit(solution)/shard_map/psum | solution.py:40
  23.0 2.8 %copy-start.9 = (s32[192]{0:T(256)S(1)}, s32[192]{0:T(256)}, u32[]{:S(2)}) copy-start(s32[192]{0:T(256)} %param.14) | copy-start | bytes 2308
  36.4 7.6 %copy-start = (bf16[192,128,64]{1,2,0:T(8,128)(2,1)}, bf16[192,128,64]{1,2,0:T(8,128)(2,1)S(1)}, u32[]{:S(2)}) copy-start(bf16[192,128,64]{1,2,0:T(8,128)(2,1)S(1)} %gather_fusion.4) | copy-start | bytes 9437188
  44.0 0.7 copy-start.6
  44.0 5.6 %copy-start.7 = (s32[4096]{0:T(1024)S(1)}, s32[4096]{0:T(1024)}, u32[]{:S(2)}) copy-start(s32[4096]{0:T(1024)} %param.11) | copy-start | bytes 49156
  44.0 30.2 %copy-start.2 = (bf16[192,128,64]{1,2,0:T(8,128)(2,1)S(1)}, bf16[192,128,64]{1,2,0:T(8,128)(2,1)}, u32[]{:S(2)}) copy-start(bf16[192,128,64]{1,2,0:T(8,128)(2,1)} %gather_fusion.5) | copy-start | bytes 9437188
  45.9 10.7 %all-to-all-start = ((bf16[16,1,128]{2,1,0:T(2,128)(2,1)}), bf16[16,1,128]{2,1,0:T(2,128)(2,1)S(1)}, u32[]{:S(2)}, u32[]{:S(2)}) async-start(bf16[16,1,128]{2,1,0:T(2,128)(2,1)} %copy.26), calls=%async_computation | async-start | bytes 16384 | tf_op jit(solution)/shard_map/all_to_all | solution.py:31
  104.8 17.7 %copy-start.1 = (bf16[192,128,64]{1,2,0:T(8,128)(2,1)S(1)}, bf16[192,128,64]{1,2,0:T(8,128)(2,1)}, u32[]{:S(2)}) copy-start(bf16[192,128,64]{1,2,0:T(8,128)(2,1)} %copy-done) | copy-start | bytes 9437188
  115.6 37.4 %all-to-all-start.2 = ((bf16[16,2,4096]{2,1,0:T(2,128)(2,1)}), bf16[16,2,4096]{2,1,0:T(2,128)(2,1)}, u32[]{:S(2)}, u32[]{:S(2)}) async-start(bf16[16,2,4096]{2,1,0:T(2,128)(2,1)} %reshape.154), calls=%async_computation.2 | async-start | bytes 524288 | tf_op jit(solution)/shard_map/all_to_all | solution.py:48
  131.9 20.0 %copy-start.5 = (f32[4096,64]{0,1:T(8,128)S(1)}, f32[4096,64]{0,1:T(8,128)}, u32[]{:S(2)}) copy-start(f32[4096,64]{0,1:T(8,128)} %param.9) | copy-start | bytes 3145732
  153.0 12.1 %copy-start.3 = (f32[6144,64]{1,0:T(8,128)S(1)}, f32[6144,64]{1,0:T(8,128)}, u32[]{:S(2)}) copy-start(f32[6144,64]{1,0:T(8,128)} %copy.36) | copy-start | bytes 4718596
Sparse Core Ops, SparseCore 0:
  44.1 29.9 all-reduce.1
where the time goes:
time: 181 us; the launch traced here: 179 us
  other arithmetic  61.6 us (34%)
  local copies, waits for them, and re-layouts  31.4 us (17%)
  matrix products  26.7 us (15%)
  waiting for transfers between devices  26.4 us (15%)
  starting transfers between devices  18.9 us (10%)
  between operations  14.3 us (8%)
    scatter-add x1, other arithmetic, body(): jnp.zeros((received, blk_rows, half_cols), jnp.float32).at[slot_of_block]  20 us
    scatter-add x1, other arithmetic, body(): jnp.zeros(id_bf.shape, jnp.float32).at[id_of_block].add(grad_right)  20 us
    psum x1, waiting for transfers between devices, body(): summed = lax.psum(partial_value, 'gy').astype(jnp.float32)  16.8 us
    unnamed x26, local copies, waits for them, and re-layouts  13.5 us
    dot_general x1, matrix products, body(): jnp.einsum('bij,bjk->bik', resid, right_rows, preferred_element_type=jnp....  9.83 us
    dot_general x1, matrix products, body(): jnp.einsum('bij,bik->bjk', resid, left_rows, preferred_element_type=jnp.f...  9.34 us
    all_to_all x1, starting transfers between devices, body(): lax.all_to_all(sent_rows, 'gx', split_axis=0, concat_axis=0, tiled=True)  8.31 us
    dot_general x1, matrix products, body(): jnp.einsum('bik,bjk->bij', left_rows, right_rows, preferred_element_type=...  7.57 us
  transfers between devices with their start and end apart: 4, of which 3 were waited for; matrix products, arithmetic and copies ran while one was open for 22% of the time, Pallas kernels for 0%

commit v1 on v0

v1 whole, which is shorter than its diff:
```python
import jax
import jax.numpy as jnp
from jax import lax
from jax.experimental import pallas as pl
from jax.experimental.pallas import tpu as pltpu
from jax.sharding import PartitionSpec as P

MESH = pl.DeviceIdType.MESH
RATE = 0.05
DECAY = 0.1
UNROLL = 4
F32 = jnp.float32
BF16 = jnp.bfloat16


def dot_nn(a, b):
    return lax.dot_general(a, b, (((1,), (0,)), ((), ())), preferred_element_type=F32)


def dot_nt(a, b):
    return lax.dot_general(a, b, (((1,), (1,)), ((), ())), preferred_element_type=F32)


def log_weight(count):
    return jnp.log(1.0 + count.astype(F32)) / jnp.log(F32(1001.0))


def exchange_kernel(
    send_list, by_slot, by_id, last_slot, last_id, rec_count, id_count,
    rec_hbm, id_hbm, obs_hbm,
    ret_out, new_id_out,
    rec, rec_bf, ids, obs, w_rec, w_id, left, right, w_right, w_left, gram,
    left_send, weight_send, weight_got, back, ret, total, total_gram,
    load_sem, ls, lr, ws, wr, fs, fr, bs, br, rs, rr,
):
    peers = lax.axis_size("gx")
    me = lax.axis_index("gx")
    half = lax.axis_index("gy")
    other = 1 - half
    idents = w_right.shape[0]
    blocks = obs.shape[0]
    blk = obs.shape[1]

    load_rec = pltpu.make_async_copy(rec_hbm, rec, load_sem.at[0])
    load_id = pltpu.make_async_copy(id_hbm, ids, load_sem.at[1])
    load_obs = pltpu.make_async_copy(obs_hbm, obs, load_sem.at[2])
    load_rec.start()
    load_id.start()
    load_obs.start()
    barrier = pltpu.get_barrier_semaphore()

    @pl.loop(1, peers)
    def _(step):
        pl.semaphore_signal(
            barrier, inc=1, device_id={"gx": lax.rem(me + step, peers)}, device_id_type=MESH
        )

    pl.semaphore_signal(barrier, inc=1, device_id={"gy": other}, device_id_type=MESH)

    weights = log_weight(rec_count[...]).astype(BF16).astype(F32)
    for r in range(weights.shape[0]):
        w_rec[r] = weights[r : r + 1, :]
    w_id[...] = log_weight(id_count[...])

    def column(block):
        return pl.ds(pl.multiple_of(block * blk, blk), blk)

    load_rec.wait()

    @pl.loop(0, rec_bf.shape[0])
    def _(r):
        rec_bf[r] = rec[:, column(r)].astype(BF16)

    @pl.loop(0, peers)
    def _(peer):
        wanted = send_list[peer]
        left_send[peer] = rec_bf[wanted]
        weight_send[peer] = w_rec[wanted]

    left[half, me] = left_send[me]
    weight_got[me] = weight_send[me]
    load_id.wait()

    @pl.loop(0, idents)
    def _(c):
        rows = ids[:, column(c)].astype(BF16)
        right[half, c] = rows
        w_right[c] = (rows.astype(F32) * w_id[pl.ds(c, 1), :]).astype(BF16)

    pl.semaphore_wait(barrier, peers)

    def left_copy(peer, slot):
        return pltpu.make_async_remote_copy(
            src_ref=left_send.at[peer], dst_ref=left.at[half, slot],
            send_sem=ls.at[peer], recv_sem=lr.at[slot],
            device_id={"gx": peer}, device_id_type=MESH,
        )

    def weight_copy(peer, slot):
        return pltpu.make_async_remote_copy(
            src_ref=weight_send.at[peer], dst_ref=weight_got.at[slot],
            send_sem=ws.at[peer], recv_sem=wr.at[slot],
            device_id={"gx": peer}, device_id_type=MESH,
        )

    def forward_copy(slot, side):
        return pltpu.make_async_remote_copy(
            src_ref=left.at[side, slot], dst_ref=left.at[side, slot],
            send_sem=fs.at[slot], recv_sem=fr.at[slot],
            device_id={"gy": other}, device_id_type=MESH,
        )

    def back_copy(peer, slot):
        return pltpu.make_async_remote_copy(
            src_ref=back.at[peer], dst_ref=ret.at[slot],
            send_sem=bs.at[peer], recv_sem=br.at[slot],
            device_id={"gx": peer}, device_id_type=MESH,
        )

    def right_copy(side):
        return pltpu.make_async_remote_copy(
            src_ref=right.at[side], dst_ref=right.at[side],
            send_sem=rs, recv_sem=rr,
            device_id={"gy": other}, device_id_type=MESH,
        )

    right_copy(half).start()

    @pl.loop(1, peers)
    def _(step):
        peer = lax.rem(me + step, peers)
        left_copy(peer, me).start()
        weight_copy(peer, me).start()

    forward_copy(me, half).start()

    right_copy(other).wait_recv()

    def full_right(c):
        return jnp.concatenate([right[0, c], right[1, c]], axis=0)

    def full_left(s):
        return jnp.concatenate([left[0, s], left[1, s]], axis=0)

    @pl.loop(0, idents)
    def _(c):
        gram[c] = dot_nt(w_right[c], full_right(c))

    load_obs.wait()

    def running_sums(order, term):
        def step(i, carry):
            acc, acc_gram = carry
            for u in range(UNROLL):
                p = i * UNROLL + u
                code = order[p]
                keep = (code >> 24).astype(F32)
                product, matrix = term((code >> 16) & 255, (code >> 8) & 255, code & 255)
                acc = acc * keep + product
                acc_gram = acc_gram * keep + matrix
                total[p] = acc
                total_gram[p] = acc_gram
            return acc, acc_gram

        zero = jnp.zeros(total.shape[1:], F32)
        lax.fori_loop(0, blocks // UNROLL, step, (zero, zero))

    running_sums(by_slot, lambda b, s, c: (dot_nt(w_right[c], obs[b]), gram[c]))

    def finish_slot(s):
        last = last_slot[s]
        weight = weight_got[s]
        both = full_left(s)
        score = dot_nn(total_gram[last].astype(BF16), both)
        back[s] = ((score - total[last]) * weight).astype(BF16)
        return weight, both

    def left_factors(s, weight, both):
        rows = (left[half, s].astype(F32) * weight).astype(BF16)
        w_left[s] = rows
        gram[s] = dot_nt(rows, both)

    @pl.loop(1, peers)
    def _(step):
        source = lax.rem(me - step + peers, peers)
        left_copy(source, source).wait_recv()
        weight_copy(source, source).wait_recv()
        forward_copy(source, half).start()

    @pl.loop(1, peers)
    def _(step):
        source = lax.rem(me - step + peers, peers)
        forward_copy(source, other).wait_recv()
        finish_slot(source)
        back_copy(source, me).start()

    forward_copy(me, other).wait_recv()
    finish_slot(me)
    ret[me] = back[me]

    @pl.loop(0, peers)
    def _(s):
        left_factors(s, weight_got[s], full_left(s))

    running_sums(by_id, lambda b, s, c: (dot_nn(w_left[s], obs[b]), gram[s]))

    @pl.loop(0, idents)
    def _(c):
        at = last_id[c] >> 1
        used = (last_id[c] & 1).astype(F32)
        score = dot_nn(total_gram[at].astype(BF16), full_right(c))
        grad = (score - total[at]) * (w_id[pl.ds(c, 1), :] * used)
        old = ids[:, column(c)]
        new_id_out[:, column(c)] = old - RATE * (grad + DECAY * old)

    @pl.loop(1, peers)
    def _(step):
        source = lax.rem(me - step + peers, peers)
        back_copy(source, source).wait_recv()

    ret_out[...] = ret[...]

    right_copy(half).wait_send()
    forward_copy(me, half).wait_send()

    @pl.loop(1, peers)
    def _(step):
        peer = lax.rem(me + step, peers)
        left_copy(peer, me).wait_send()
        weight_copy(peer, me).wait_send()
        forward_copy(peer, half).wait_send()
        back_copy(peer, me).wait_send()


def exchange(send_list, by_slot, by_id, last_slot, last_id, rec_count, id_count, rec_t, id_t, obs):
    peers = lax.axis_size("gx")
    half_cols = rec_t.shape[0]
    blocks, blk, _ = obs.shape
    idents = id_count.shape[0]
    smem = pl.BlockSpec(memory_space=pltpu.SMEM)
    vmem = pl.BlockSpec(memory_space=pltpu.VMEM)
    hbm = pl.BlockSpec(memory_space=pl.ANY)
    dma = pltpu.SemaphoreType.DMA
    return pl.pallas_call(
        exchange_kernel,
        out_shape=(
            jax.ShapeDtypeStruct((peers, half_cols, blk), BF16),
            jax.ShapeDtypeStruct(id_t.shape, F32),
        ),
        in_specs=[smem] * 5 + [vmem] * 2 + [hbm] * 3,
        out_specs=(vmem, vmem),
        scratch_shapes=[
            pltpu.VMEM(rec_t.shape, F32),
            pltpu.VMEM((rec_count.shape[0], half_cols, blk), BF16),
            pltpu.VMEM(id_t.shape, F32),
            pltpu.VMEM(obs.shape, BF16),
            pltpu.VMEM((rec_count.shape[0], 1, blk), F32),
            pltpu.VMEM(id_count.shape, F32),
            pltpu.VMEM((2, peers, half_cols, blk), BF16),
            pltpu.VMEM((2, idents, half_cols, blk), BF16),
            pltpu.VMEM((idents, half_cols, blk), BF16),
            pltpu.VMEM((peers, half_cols, blk), BF16),
            pltpu.VMEM((max(idents, peers), half_cols, 2 * half_cols), F32),
            pltpu.VMEM((peers, half_cols, blk), BF16),
            pltpu.VMEM((peers, 1, blk), F32),
            pltpu.VMEM((peers, 1, blk), F32),
            pltpu.VMEM((peers, half_cols, blk), BF16),
            pltpu.VMEM((peers, half_cols, blk), BF16),
            pltpu.VMEM((blocks, half_cols, blk), F32),
            pltpu.VMEM((blocks, half_cols, 2 * half_cols), F32),
            dma((3,)),
        ]
        + [dma((peers,))] * 8
        + [dma, dma],
        compiler_params=pltpu.CompilerParams(
            collective_id=0, has_side_effects=True, vmem_limit_bytes=56 << 20
        ),
        name="exchange",
    )(send_list, by_slot, by_id, last_slot, last_id, rec_count, id_count, rec_t, id_t, obs)


def update_kernel(send_list, rec, ret, new_id, new_rec, id_out, sem):
    blk = ret.shape[2]
    pass_on = pltpu.make_async_copy(new_id, id_out, sem)
    pass_on.start()
    old = rec[...]
    new_rec[...] = old - (RATE * DECAY) * old

    @pl.loop(0, ret.shape[0])
    def _(s):
        cols = pl.ds(pl.multiple_of(send_list[s] * blk, blk), blk)
        new_rec[:, cols] = new_rec[:, cols] - RATE * ret[s].astype(F32)

    pass_on.wait()


def update(send_list, rec_t, ret, new_id):
    vmem = pl.BlockSpec(memory_space=pltpu.VMEM)
    hbm = pl.BlockSpec(memory_space=pl.ANY)
    return pl.pallas_call(
        update_kernel,
        out_shape=(
            jax.ShapeDtypeStruct(rec_t.shape, F32),
            jax.ShapeDtypeStruct(new_id.shape, F32),
        ),
        in_specs=[pl.BlockSpec(memory_space=pltpu.SMEM), vmem, vmem, hbm],
        out_specs=(vmem, hbm),
        scratch_shapes=[pltpu.SemaphoreType.DMA],
        compiler_params=pltpu.CompilerParams(vmem_limit_bytes=32 << 20),
        name="update",
    )(send_list, rec_t, ret, new_id)


def body(records, idents, rec_count, id_count, observed, send_list, slot_of_block, id_of_block):
    peers = lax.axis_size("gx")
    blocks, blk, _ = observed.shape
    id_blocks = idents.shape[0] // blk
    wanted = send_list.reshape(-1)
    place = jnp.arange(blocks, dtype=jnp.int32)
    code = (place << 16) | (slot_of_block << 8) | id_of_block

    def in_order(key):
        same = key[None, :] == key[:, None]
        ahead = place[None, :] < place[:, None]
        earlier = jnp.sum((same & ahead).astype(jnp.int32), axis=1)
        rank = earlier + jnp.sum((key[None, :] < key[:, None]).astype(jnp.int32), axis=1)
        marked = code | (jnp.minimum(earlier, 1) << 24)
        return jnp.sum(jnp.where(rank[:, None] == place[None, :], marked[:, None], 0), axis=0)

    def up_to(key, count):
        below = key[:, None] <= jnp.arange(count, dtype=jnp.int32)[None, :]
        return jnp.sum(below.astype(jnp.int32), axis=0)

    def uses(key, count):
        equal = key[:, None] == jnp.arange(count, dtype=jnp.int32)[None, :]
        return jnp.sum(equal.astype(jnp.int32), axis=0)

    last_slot = up_to(slot_of_block, peers) - 1
    last_id = jnp.maximum(up_to(id_of_block, id_blocks) - 1, 0) * 2
    last_id = last_id + jnp.minimum(uses(id_of_block, id_blocks), 1)
    ret, new_id = exchange(
        wanted,
        in_order(slot_of_block),
        in_order(id_of_block),
        last_slot,
        last_id,
        rec_count.reshape(-1, blk),
        id_count.reshape(-1, blk),
        records.T,
        idents.T,
        observed,
    )
    new_rec, new_id = update(wanted, records.T, ret, new_id)
    return new_rec.T, new_id.T


def solution(mesh):
    in_specs = (
        P("gx", "gy"),
        P("gx", "gy"),
        P("gx"),
        P("gx"),
        P("gx", None, None),
        P("gx", None),
        P("gx"),
        P("gx"),
    )
    out_specs = (P("gx", "gy"), P("gx", "gy"))
    return jax.shard_map(body, mesh=mesh, in_specs=in_specs, out_specs=out_specs, check_vma=False)
```

time: 181 us -> 56.8 us (0.31)
  other arithmetic: 61.6 us -> 6.08 us
  Pallas kernels: 0 us -> 47.5 us
  local copies, waits for them, and re-layouts: 31.4 us -> 2.17 us
  matrix products: 26.7 us -> 0 us
  waiting for transfers between devices: 26.4 us -> 0 us
  starting transfers between devices: 18.9 us -> 0 us
  between operations: 14.3 us -> 0.67 us
    pallas_call x0 -> x2, Pallas kernels: none -> 47.5 us  [the longest x1 44.8 us: exchange(): pl.pallas_call(exchange_kernel, out_shape=(jax.ShapeDtypeStruct((peers, h...]
    scatter-add x3 -> x0, other arithmetic: 43.2 us -> none  [the longest x1 20 us: body(): jnp.zeros((received, blk_rows, half_cols), jnp.float32).at[slot_of_block]]
    dot_general x3 -> x0, matrix products: 26.7 us -> none  [the longest x1 9.83 us: body(): jnp.einsum('bij,bjk->bik', resid, right_rows, preferred_element_type=jnp....]
    all_to_all x3 -> x0, starting transfers between devices: 18.8 us -> none  [the longest x1 8.31 us: body(): lax.all_to_all(sent_rows, 'gx', split_axis=0, concat_axis=0, tiled=True)]
    psum x1 -> x0, waiting for transfers between devices: 16.8 us -> none  [body(): summed = lax.psum(partial_value, 'gy').astype(jnp.float32)]
    unnamed x26 -> x8, local copies, waits for them, and re-layouts: 13.5 us -> 2.17 us
    all_to_all x3 -> x0, waiting for transfers between devices: 9.59 us -> none  [the longest x1 6.87 us: body(): lax.all_to_all(sent_rows, 'gx', split_axis=0, concat_axis=0, tiled=True)]
    gather x8 -> x0, local copies, waits for them, and re-layouts: 7.37 us -> none  [the longest x1 2.75 us: body(): right_rows = id_bf[id_of_block]]
  transfers between devices with their start and end apart: 4 -> 0, of which waited for: 3 -> 0; matrix products, arithmetic and copies ran while one was open for 22% -> 0% of each run, Pallas kernels for 0% -> 0%
where the time goes in v1:
time: 56.8 us; the launch traced here: 56.4 us
  Pallas kernels  47.5 us (84%)
  other arithmetic  6.08 us (11%)
  local copies, waits for them, and re-layouts  2.17 us (4%)
  between operations  0.67 us (1%)
    pallas_call x1, Pallas kernels, exchange(): pl.pallas_call(exchange_kernel, out_shape=(jax.ShapeDtypeStruct((peers, h...  44.8 us
    pallas_call x1, Pallas kernels, update(): pl.pallas_call(update_kernel, out_shape=(jax.ShapeDtypeStruct(rec_t.shape...  2.66 us
    unnamed x8, local copies, waits for them, and re-layouts  2.17 us
    reduce_sum x2, other arithmetic, in_order(): jnp.sum((key[None, :] < key[:, None]).astype(jnp.int32), axis=1)  1.95 us
    reduce_sum x2, other arithmetic, up_to(): return jnp.sum(below.astype(jnp.int32), axis=0)  1.59 us

profile of v1, /device:TPU:0, one launch (start us, length us, event | category | flops | bytes accessed | tf_op | source)
XLA Modules:
  0.0 56.4 jit_solution(9615745563534379101)
XLA Ops:
  0.6 0.8 %convert_reduce_fusion.6 = s32[16]{0:T(128)S(1)} fusion(s32[192]{0:T(256)} %param.14), kind=kLoop, calls=%fused_computation.15 | loop fusion | flops 9200 | bytes 832 | tf_op jit(solution)/shard_map/reduce_sum | solution.py:332
  1.4 0.6 broadcast_add_fusion.last_slot
  2.0 0.8 %convert_reduce_fusion.5 = (s32[32]{0:T(128)S(1)}, s32[32]{0:T(128)S(1)}) fusion(s32[192]{0:T(256)} %param.15), kind=kLoop, calls=%fused_computation.13 | loop fusion | flops 36800 | bytes 1024 | tf_op jit(solution)/shard_map/reduce_sum | solution.py:332
  2.8 0.5 minimum_add_fusion.last_id
  3.3 1.0 %convert_reduce_fusion.2 = (s32[192]{0:T(256)S(1)}, s32[192]{0:T(256)S(1)}) fusion(s32[192]{0:T(256)} %param.14), kind=kLoop, calls=%fused_computation.6 | loop fusion | flops 294528 | bytes 2304 | tf_op jit(solution)/shard_map/reduce_sum | solution.py:326
  4.3 1.0 %convert_reduce_fusion = (s32[192]{0:T(256)S(1)}, s32[192]{0:T(256)S(1)}) fusion(s32[192]{0:T(256)} %param.15), kind=kLoop, calls=%fused_computation.2 | loop fusion | flops 294528 | bytes 2304 | tf_op jit(solution)/shard_map/reduce_sum | solution.py:326
  5.3 0.7 %shift-left_or_fusion = (s32[192]{0:T(256)S(1)}, s32[192]{0:T(256)S(1)}, s32[192]{0:T(256)S(1)}, s32[192]{0:T(256)S(1)}) fusion(s32[192]{0:T(256)S(1)} %get-tuple-element.13, s32[192]{0:T(256)} %param.15, s32[192]{0:T(256)} %param.14, s32[192]{0:T(256)S(1)} %get-tuple-element.15, s32[192]{0:T(256)S(1)} %get-tuple-element.14, s32[192]{0:T(256)S(1)} %get-tuple-element.12), kind=kLoop, calls=%fused_computation.17 | loop fusion | flops 2304 | bytes 7680 | tf_op jit(solution)/shard_map/or | solution.py:327
  6.0 0.7 %select_reduce_fusion = (s32[192]{0:T(256)}, s32[192]{0:T(256)}) fusion(s32[192]{0:T(256)S(1)} %get-tuple-element.16, s32[192]{0:T(256)S(1)} %get-tuple-element.19, s32[192]{0:T(256)S(1)} %get-tuple-element.17, s32[192]{0:T(256)S(1)} %get-tuple-element.18), kind=kLoop, calls=%fused_computation | loop fusion | flops 220800 | bytes 4608 | tf_op jit(solution)/shard_map/reduce_sum | solution.py:328
  6.7 0.0 copy-start
  6.7 0.0 copy-start.3
  6.7 44.8 %exchange.1 = (bf16[16,64,128]{2,1,0:T(8,128)(2,1)}, f32[64,4096]{1,0:T(8,128)}) custom-call(s32[16]{0:T(128)} %bitcast.9, s32[192]{0:T(256)} %get-tuple-element.21.by_slot, s32[192]{0:T(256)} %get-tuple-element.20.by_id, s32[16]{0:T(128)} %broadcast_add_fusion.last_slot, s32[32]{0:T(128)} %minimum_add_fusion.last_id, s32[48,128]{1,0:T(8,128)} %bitcast.12, ...), custom_call_target="tpu_custom_call" | custom-call | tf_op jit(solution)/shard_map/exchange/pallas_call | solution.py:244
  51.5 0.0 copy-done
  51.6 0.0 copy-done.3
  51.6 0.0 copy-start.1
  51.6 1.2 %copy-done.1 = f32[64,4096]{1,0:T(8,128)S(1)} copy-done((f32[64,4096]{1,0:T(8,128)S(1)}, f32[64,4096]{1,0:T(8,128)}, u32[]{:S(2)}) %copy-start.1) | copy-done | bytes 1048600
  52.8 0.0 copy-start.2
  52.8 0.9 %copy-done.2 = bf16[16,64,128]{2,1,0:T(8,128)(2,1)S(1)} copy-done((bf16[16,64,128]{2,1,0:T(8,128)(2,1)S(1)}, bf16[16,64,128]{2,1,0:T(8,128)(2,1)}, u32[]{:S(2)}) %copy-start.2) | copy-done | bytes 262168
  53.7 2.7 %update.1 = (f32[64,6144]{1,0:T(8,128)}, f32[64,4096]{1,0:T(8,128)}) custom-call(s32[16]{0:T(128)S(1)} %bitcast.10, f32[64,6144]{1,0:T(8,128)S(1)} %bitcast.8, bf16[16,64,128]{2,1,0:T(8,128)(2,1)S(1)} %copy-done.2, f32[64,4096]{1,0:T(8,128)S(1)} %copy-done.1), custom_call_target="tpu_custom_call" | custom-call | tf_op jit(solution)/shard_map/update/pallas_call | solution.py:300
Async XLA Ops:
  6.7 44.8 %copy-start = (f32[6144,64]{0,1:T(8,128)S(1)}, f32[6144,64]{0,1:T(8,128)}, u32[]{:S(2)}) copy-start(f32[6144,64]{0,1:T(8,128)} %param.8) | copy-start | bytes 4718596
  6.7 44.8 %copy-start.3 = (s32[16,1]{0,1:T(1,128)S(1)}, s32[16,1]{0,1:T(1,128)}, u32[]{:S(2)}) copy-start(s32[16,1]{0,1:T(1,128)} %param.13) | copy-start | bytes 196
  51.6 1.2 %copy-start.1 = (f32[64,4096]{1,0:T(8,128)S(1)}, f32[64,4096]{1,0:T(8,128)}, u32[]{:S(2)}) copy-start(f32[64,4096]{1,0:T(8,128)} %get-tuple-element.7.new_id) | copy-start | bytes 3145732
  52.8 0.9 %copy-start.2 = (bf16[16,64,128]{2,1,0:T(8,128)(2,1)S(1)}, bf16[16,64,128]{2,1,0:T(8,128)(2,1)}, u32[]{:S(2)}) copy-start(bf16[16,64,128]{2,1,0:T(8,128)(2,1)} %get-tuple-element.6.ret) | copy-start | bytes 786436

commit v2 on v1

v2 whole, which is shorter than its diff:
```python
import jax
import jax.numpy as jnp
from jax import lax
from jax.experimental import pallas as pl
from jax.experimental.pallas import tpu as pltpu
from jax.sharding import PartitionSpec as P

MESH = pl.DeviceIdType.MESH
RATE = 0.05
DECAY = 0.1
UNROLL = 16
GROUP = 4
LANES = 256
F32 = jnp.float32
BF16 = jnp.bfloat16


def dot_nn(a, b):
    return lax.dot_general(a, b, (((1,), (0,)), ((), ())), preferred_element_type=F32)


def dot_nt(a, b):
    return lax.dot_general(a, b, (((1,), (1,)), ((), ())), preferred_element_type=F32)


def log_weight(count):
    return jnp.log(1.0 + count.astype(F32)) / jnp.log(F32(1001.0))


def column_of(row):
    size = row.shape[1]
    diagonal = lax.broadcasted_iota(jnp.int32, (size, size), 0) == lax.broadcasted_iota(
        jnp.int32, (size, size), 1
    )
    return jnp.sum(jnp.where(diagonal, row, 0.0), axis=1, keepdims=True)


def sorted_codes(key, payload):
    size = key.shape[1]
    across = lax.broadcasted_iota(jnp.int32, (size, size), 1)
    ahead = across < lax.broadcasted_iota(jnp.int32, (size, size), 0)
    key_col = column_of(key)
    earlier = jnp.sum(jnp.where((key == key_col) & ahead, 1.0, 0.0), axis=1, keepdims=True)
    rank = earlier + jnp.sum(jnp.where(key < key_col, 1.0, 0.0), axis=1, keepdims=True)
    marked = 2.0 * column_of(payload) + jnp.minimum(earlier, 1.0)
    order = jnp.sum(jnp.where(rank == across.astype(F32), marked, 0.0), axis=0, keepdims=True)
    value = lax.broadcasted_iota(jnp.int32, (1, LANES), 1).astype(F32)
    up_to = jnp.sum(jnp.where(key_col <= value, 1.0, 0.0), axis=0, keepdims=True)
    used = jnp.sum(jnp.where(key_col == value, 1.0, 0.0), axis=0, keepdims=True)
    last = 2.0 * jnp.maximum(up_to - 1.0, 0.0) + jnp.minimum(used, 1.0)
    return order.astype(jnp.int32), last.astype(jnp.int32)


def exchange_kernel(
    send_list, send_row, slot_row, id_row, rec_count, id_count,
    rec_hbm, id_hbm, obs_hbm,
    new_rec_out, new_id_out,
    rec, rec_bf, ids, new_ids, obs, w_rec, w_id, left, right, w_right, w_left, gram,
    left_send, weight_send, weight_got, back, ret, total, total_gram,
    plan, plan_smem, load_sem, ls, lr, ws, wr, fs, fr, bs, br, rs, rr,
):
    peers = lax.axis_size("gx")
    me = lax.axis_index("gx")
    half = lax.axis_index("gy")
    other = 1 - half
    idents = w_right.shape[0]
    blocks = obs.shape[0]
    blk = obs.shape[1]

    load_rec = pltpu.make_async_copy(rec_hbm, rec, load_sem.at[0])
    load_id = pltpu.make_async_copy(id_hbm, ids, load_sem.at[1])
    load_obs = pltpu.make_async_copy(obs_hbm, obs, load_sem.at[2])
    load_rec.start()
    load_id.start()
    load_obs.start()
    barrier = pltpu.get_barrier_semaphore()

    @pl.loop(1, peers)
    def _(step):
        pl.semaphore_signal(
            barrier, inc=1, device_id={"gx": lax.rem(me + step, peers)}, device_id_type=MESH
        )

    pl.semaphore_signal(barrier, inc=1, device_id={"gy": other}, device_id_type=MESH)

    weights = log_weight(rec_count[...]).astype(BF16).astype(F32)
    for r in range(weights.shape[0]):
        w_rec[r] = weights[r : r + 1, :]
    w_id[...] = log_weight(id_count[...])

    place = lax.broadcasted_iota(jnp.int32, (1, blocks), 1)
    code = ((place * 128 + slot_row[...]) * 32 + id_row[...]).astype(F32)
    slots = lax.broadcasted_iota(jnp.int32, (1, peers), 1).astype(F32)
    for row, key, payload in (
        (0, slot_row[...].astype(F32), code),
        (2, id_row[...].astype(F32), code),
        (4, send_row[...].astype(F32), slots),
    ):
        order, last = sorted_codes(key, payload)
        plan[row : row + 1, : order.shape[1]] = order
        plan[row + 1 : row + 2, :] = last
    plan_copy = pltpu.make_async_copy(plan, plan_smem, load_sem.at[3])
    plan_copy.start()

    def within(index, count):
        return jnp.clip(index, 0, count - 1)

    def column(block):
        return pl.ds(pl.multiple_of(block * blk, blk), blk)

    def unrolled(count, function):
        @pl.loop(0, count // GROUP)
        def _(i):
            for u in range(GROUP):
                function(i * GROUP + u)

    load_rec.wait()

    def round_record(r):
        rec_bf[r] = rec[:, column(r)].astype(BF16)

    unrolled(rec_bf.shape[0], round_record)

    @pl.loop(0, peers)
    def _(peer):
        wanted = send_list[peer]
        left_send[peer] = rec_bf[wanted]
        weight_send[peer] = w_rec[wanted]

    left[half, me] = left_send[me]
    weight_got[me] = weight_send[me]
    load_id.wait()

    def round_ident(c):
        rows = ids[:, column(c)].astype(BF16)
        right[half, c] = rows
        w_right[c] = (rows.astype(F32) * w_id[pl.ds(c, 1), :]).astype(BF16)

    unrolled(idents, round_ident)
    pl.semaphore_wait(barrier, peers)

    def left_copy(peer, slot):
        return pltpu.make_async_remote_copy(
            src_ref=left_send.at[peer], dst_ref=left.at[half, slot],
            send_sem=ls.at[peer], recv_sem=lr.at[slot],
            device_id={"gx": peer}, device_id_type=MESH,
        )

    def weight_copy(peer, slot):
        return pltpu.make_async_remote_copy(
            src_ref=weight_send.at[peer], dst_ref=weight_got.at[slot],
            send_sem=ws.at[peer], recv_sem=wr.at[slot],
            device_id={"gx": peer}, device_id_type=MESH,
        )

    def forward_copy(slot, side):
        return pltpu.make_async_remote_copy(
            src_ref=left.at[side, slot], dst_ref=left.at[side, slot],
            send_sem=fs.at[slot], recv_sem=fr.at[slot],
            device_id={"gy": other}, device_id_type=MESH,
        )

    def back_copy(peer, slot):
        return pltpu.make_async_remote_copy(
            src_ref=back.at[peer], dst_ref=ret.at[slot],
            send_sem=bs.at[peer], recv_sem=br.at[slot],
            device_id={"gx": peer}, device_id_type=MESH,
        )

    def right_copy(side):
        return pltpu.make_async_remote_copy(
            src_ref=right.at[side], dst_ref=right.at[side],
            send_sem=rs, recv_sem=rr,
            device_id={"gy": other}, device_id_type=MESH,
        )

    right_copy(half).start()

    @pl.loop(1, peers)
    def _(step):
        peer = lax.rem(me + step, peers)
        left_copy(peer, me).start()
        weight_copy(peer, me).start()

    forward_copy(me, half).start()

    right_copy(other).wait_recv()

    def full_right(c):
        return jnp.concatenate([right[0, c], right[1, c]], axis=0)

    def full_left(s):
        return jnp.concatenate([left[0, s], left[1, s]], axis=0)

    def right_gram(c):
        gram[c] = dot_nt(w_right[c], full_right(c))

    unrolled(idents, right_gram)
    load_obs.wait()
    plan_copy.wait()

    def running_sums(row, term):
        def step(i, carry):
            acc, acc_gram = carry
            for u in range(UNROLL):
                p = i * UNROLL + u
                code = plan_smem[row, p]
                keep = (code & 1).astype(F32)
                product, matrix = term(
                    within(code >> 13, blocks), within((code >> 6) & 127, peers), (code >> 1) & 31
                )
                acc = acc * keep + product
                acc_gram = acc_gram * keep + matrix
                total[p] = acc
                total_gram[p] = acc_gram
            return acc, acc_gram

        zero = jnp.zeros(total.shape[1:], F32)
        lax.fori_loop(0, blocks // UNROLL, step, (zero, zero))

    running_sums(0, lambda b, s, c: (dot_nt(w_right[c], obs[b]), gram[c]))

    def finish_slot(s):
        last = within(plan_smem[1, s] >> 1, blocks)
        score = dot_nn(total_gram[last].astype(BF16), full_left(s))
        back[s] = ((score - total[last]) * weight_got[s]).astype(BF16)

    def left_factors(s):
        rows = (left[half, s].astype(F32) * weight_got[s]).astype(BF16)
        w_left[s] = rows
        gram[s] = dot_nt(rows, full_left(s))

    @pl.loop(1, peers)
    def _(step):
        source = lax.rem(me - step + peers, peers)
        left_copy(source, source).wait_recv()
        weight_copy(source, source).wait_recv()
        forward_copy(source, half).start()

    @pl.loop(0, peers // GROUP)
    def _(i):
        sources = [lax.rem(me - (i * GROUP + u) + peers, peers) for u in range(GROUP)]
        for source in sources:
            forward_copy(source, other).wait_recv()
        for source in sources:
            finish_slot(source)
        for u, source in enumerate(sources):
            if u > 0:
                back_copy(source, me).start()
            else:

                @pl.when(i > 0)
                def _():
                    back_copy(source, me).start()

    ret[me] = back[me]
    unrolled(peers, left_factors)
    running_sums(2, lambda b, s, c: (dot_nn(w_left[s], obs[b]), gram[s]))

    def finish_ident(c):
        at = within(plan_smem[3, c] >> 1, blocks)
        used = (plan_smem[3, c] & 1).astype(F32)
        score = dot_nn(total_gram[at].astype(BF16), full_right(c))
        grad = (score - total[at]) * (w_id[pl.ds(c, 1), :] * used)
        old = ids[:, column(c)]
        new_ids[:, column(c)] = old - RATE * (grad + DECAY * old)

    unrolled(idents, finish_ident)
    store_id = pltpu.make_async_copy(new_ids, new_id_out, load_sem.at[1])
    store_id.start()

    @pl.loop(1, peers)
    def _(step):
        source = lax.rem(me - step + peers, peers)
        back_copy(source, source).wait_recv()

    def add_returned(p, acc):
        code = plan_smem[4, p]
        acc = acc * (code & 1).astype(F32) + ret[within(code >> 1, peers)].astype(F32)
        total[p] = acc
        return acc

    lax.fori_loop(0, peers, add_returned, jnp.zeros(total.shape[1:], F32))

    def finish_record(r):
        at = within(plan_smem[5, r] >> 1, blocks)
        used = (plan_smem[5, r] & 1).astype(F32)
        old = rec[:, column(r)]
        rec[:, column(r)] = old - RATE * (total[at] * used + DECAY * old)

    unrolled(rec_bf.shape[0], finish_record)
    store_rec = pltpu.make_async_copy(rec, new_rec_out, load_sem.at[0])
    store_rec.start()

    right_copy(half).wait_send()
    forward_copy(me, half).wait_send()

    @pl.loop(1, peers)
    def _(step):
        peer = lax.rem(me + step, peers)
        left_copy(peer, me).wait_send()
        weight_copy(peer, me).wait_send()
        forward_copy(peer, half).wait_send()
        back_copy(peer, me).wait_send()

    store_id.wait()
    store_rec.wait()


def exchange(send_list, slot_of_block, id_of_block, rec_count, id_count, rec_t, id_t, obs):
    peers = lax.axis_size("gx")
    half_cols = rec_t.shape[0]
    blocks, blk, _ = obs.shape
    idents = id_count.shape[0]
    smem = pl.BlockSpec(memory_space=pltpu.SMEM)
    vmem = pl.BlockSpec(memory_space=pltpu.VMEM)
    hbm = pl.BlockSpec(memory_space=pl.ANY)
    dma = pltpu.SemaphoreType.DMA
    return pl.pallas_call(
        exchange_kernel,
        out_shape=(
            jax.ShapeDtypeStruct(rec_t.shape, F32),
            jax.ShapeDtypeStruct(id_t.shape, F32),
        ),
        in_specs=[smem] + [vmem] * 5 + [hbm] * 3,
        out_specs=(hbm, hbm),
        scratch_shapes=[
            pltpu.VMEM(rec_t.shape, F32),
            pltpu.VMEM((rec_count.shape[0], half_cols, blk), BF16),
            pltpu.VMEM(id_t.shape, F32),
            pltpu.VMEM(id_t.shape, F32),
            pltpu.VMEM(obs.shape, BF16),
            pltpu.VMEM((rec_count.shape[0], 1, blk), F32),
            pltpu.VMEM(id_count.shape, F32),
            pltpu.VMEM((2, peers, half_cols, blk), BF16),
            pltpu.VMEM((2, idents, half_cols, blk), BF16),
            pltpu.VMEM((idents, half_cols, blk), BF16),
            pltpu.VMEM((peers, half_cols, blk), BF16),
            pltpu.VMEM((max(idents, peers), half_cols, 2 * half_cols), F32),
            pltpu.VMEM((peers, half_cols, blk), BF16),
            pltpu.VMEM((peers, 1, blk), F32),
            pltpu.VMEM((peers, 1, blk), F32),
            pltpu.VMEM((peers, half_cols, blk), BF16),
            pltpu.VMEM((peers, half_cols, blk), BF16),
            pltpu.VMEM((blocks, half_cols, blk), F32),
            pltpu.VMEM((blocks, half_cols, 2 * half_cols), F32),
            pltpu.VMEM((8, LANES), jnp.int32),
            pltpu.SMEM((8, LANES), jnp.int32),
            dma((4,)),
        ]
        + [dma((peers,))] * 8
        + [dma, dma],
        compiler_params=pltpu.CompilerParams(
            collective_id=0, has_side_effects=True, vmem_limit_bytes=56 << 20
        ),
        name="exchange",
    )(
        send_list, send_list[None], slot_of_block[None], id_of_block[None],
        rec_count, id_count, rec_t, id_t, obs,
    )


def body(records, idents, rec_count, id_count, observed, send_list, slot_of_block, id_of_block):
    blk = observed.shape[1]
    new_rec, new_id = exchange(
        send_list.reshape(-1),
        slot_of_block,
        id_of_block,
        rec_count.reshape(-1, blk),
        id_count.reshape(-1, blk),
        records.T,
        idents.T,
        observed,
    )
    return new_rec.T, new_id.T


def solution(mesh):
    in_specs = (
        P("gx", "gy"),
        P("gx", "gy"),
        P("gx"),
        P("gx"),
        P("gx", None, None),
        P("gx", None),
        P("gx"),
        P("gx"),
    )
    out_specs = (P("gx", "gy"), P("gx", "gy"))
    return jax.shard_map(body, mesh=mesh, in_specs=in_specs, out_specs=out_specs, check_vma=False)
```

time: 56.8 us -> 33 us (0.58)
  Pallas kernels: 47.5 us -> 28.4 us
  other arithmetic: 6.08 us -> 0 us
  local copies, waits for them, and re-layouts: 2.17 us -> 3.73 us
    pallas_call x2 -> x1, Pallas kernels: 47.5 us -> 28.4 us  [exchange(): pl.pallas_call(exchange_kernel, out_shape=(jax.ShapeDtypeStruct(rec_t.sha...]
    reduce_sum x5 -> x0, other arithmetic: 4.29 us -> none  [the longest x2 1.95 us: in_order(): jnp.sum((key[None, :] < key[:, None]).astype(jnp.int32), axis=1)]
    unnamed x8 -> x4, local copies, waits for them, and re-layouts: 2.17 us -> 3.73 us
    or x1 -> x0, other arithmetic: 0.71 us -> none  [in_order(): marked = code | jnp.minimum(earlier, 1) << 24]
where the time goes in v2:
time: 33 us; the launch traced here: 32.8 us
  Pallas kernels  28.4 us (86%)
  local copies, waits for them, and re-layouts  3.73 us (11%)
  between operations  0.65 us (2%)
    pallas_call x1, Pallas kernels, exchange(): pl.pallas_call(exchange_kernel, out_shape=(jax.ShapeDtypeStruct(rec_t.sha...  28.4 us
    unnamed x4, local copies, waits for them, and re-layouts  3.73 us

profile of v2, /device:TPU:0, one launch (start us, length us, event | category | flops | bytes accessed | tf_op | source)
XLA Modules:
  0.0 32.8 jit_solution(7690072983810856440)
XLA Ops:
  0.6 28.4 %exchange.1 = (f32[64,6144]{1,0:T(8,128)}, f32[64,4096]{1,0:T(8,128)}) custom-call(s32[16]{0:T(128)} %bitcast.16, s32[1,16]{1,0:T(1,128)} %bitcast.17, s32[1,192]{1,0:T(1,128)} %bitcast.18, s32[1,192]{1,0:T(1,128)} %bitcast.19, s32[48,128]{1,0:T(8,128)} %bitcast.14, s32[32,128]{1,0:T(8,128)} %bitcast.15, f32[64,6144]{1,0:T(8,128)} %bitcast.10, ...), custom_call_target="tpu_custom_call" | custom-call | tf_op jit(solution)/shard_map/exchange/pallas_call | solution.py:319
  29.0 0.0 copy-start
  29.0 2.8 %copy.12 = f32[6144,64]{0,1:T(8,128)} copy(f32[6144,64]{0,1:T(8,128)} %bitcast.11) | data formatting | bytes 3145728
  31.8 0.0 copy-done
  31.8 1.0 %copy.13 = f32[4096,64]{0,1:T(8,128)} copy(f32[4096,64]{0,1:T(8,128)S(1)} %bitcast.13) | data formatting | bytes 2097152
Async XLA Ops:
  29.0 2.8 %copy-start = (f32[64,4096]{1,0:T(8,128)S(1)}, f32[64,4096]{1,0:T(8,128)}, u32[]{:S(2)}) copy-start(f32[64,4096]{1,0:T(8,128)} %get-tuple-element.5) | copy-start | bytes 3145732

commit v3 on v2

--- a/solution.py
+++ b/solution.py
@@ -10,6 +10,7 @@
 DECAY = 0.1
 UNROLL = 16
 GROUP = 4
+PARTS = 4
 LANES = 256
 F32 = jnp.float32
 BF16 = jnp.bfloat16
@@ -52,9 +53,9 @@
 
 
 def exchange_kernel(
-    send_list, send_row, slot_row, id_row, rec_count, id_count,
+    send_list, slot_row, id_row, rec_count, id_count,
     rec_hbm, id_hbm, obs_hbm,
-    new_rec_out, new_id_out,
+    ret_out, new_id_out,
     rec, rec_bf, ids, new_ids, obs, w_rec, w_id, left, right, w_right, w_left, gram,
     left_send, weight_send, weight_got, back, ret, total, total_gram,
     plan, plan_smem, load_sem, ls, lr, ws, wr, fs, fr, bs, br, rs, rr,
@@ -72,7 +73,6 @@
     load_obs = pltpu.make_async_copy(obs_hbm, obs, load_sem.at[2])
     load_rec.start()
     load_id.start()
-    load_obs.start()
     barrier = pltpu.get_barrier_semaphore()
 
     @pl.loop(1, peers)
@@ -86,15 +86,95 @@
     weights = log_weight(rec_count[...]).astype(BF16).astype(F32)
     for r in range(weights.shape[0]):
         w_rec[r] = weights[r : r + 1, :]
+
+    def within(index, count):
+        return jnp.clip(index, 0, count - 1)
+
+    def column(block):
+        return pl.ds(pl.multiple_of(block * blk, blk), blk)
+
+    def unrolled(count, function):
+        @pl.loop(0, count // GROUP)
+        def _(i):
+            for u in range(GROUP):
+                function(i * GROUP + u)
+
+    load_rec.wait()
+    load_obs.start()
+
+    def round_record(r):
+        rec_bf[r] = rec[:, column(r)].astype(BF16)
+
+    unrolled(rec_bf.shape[0], round_record)
+
+    @pl.loop(0, peers)
+    def _(peer):
+        wanted = send_list[peer]
+        left_send[peer] = rec_bf[wanted]
+        weight_send[peer] = w_rec[wanted]
+
+    left[half, me] = left_send[me]
+    weight_got[me] = weight_send[me]
+    pl.semaphore_wait(barrier, peers)
+
+    def left_copy(peer, slot):
+        return pltpu.make_async_remote_copy(
+            src_ref=left_send.at[peer], dst_ref=left.at[half, slot],
+            send_sem=ls.at[peer], recv_sem=lr.at[slot],
+            device_id={"gx": peer}, device_id_type=MESH,
+        )
+
+    def weight_copy(peer, slot):
+        return pltpu.make_async_remote_copy(
+            src_ref=weight_send.at[peer], dst_ref=weight_got.at[slot],
+            send_sem=ws.at[peer], recv_sem=wr.at[slot],
+            device_id={"gx": peer}, device_id_type=MESH,
+        )
+
+    def forward_copy(slot, side):
+        return pltpu.make_async_remote_copy(
+            src_ref=left.at[side, slot], dst_ref=left.at[side, slot],
+            send_sem=fs.at[slot], recv_sem=fr.at[slot],
+            device_id={"gy": other}, device_id_type=MESH,
+        )
+
+    def back_copy(peer, slot):
+        return pltpu.make_async_remote_copy(
+            src_ref=back.at[peer], dst_ref=ret.at[slot],
+            send_sem=bs.at[peer], recv_sem=br.at[slot],
+            device_id={"gx": peer}, device_id_type=MESH,
+        )
+
+    def right_copy(side):
+        return pltpu.make_async_remote_copy(
+            src_ref=right.at[side], dst_ref=right.at[side],
+            send_sem=rs, recv_sem=rr,
+            device_id={"gy": other}, device_id_type=MESH,
+        )
+
+    @pl.loop(1, peers)
+    def _(step):
+        peer = lax.rem(me + step, peers)
+        left_copy(peer, me).start()
+        weight_copy(peer, me).start()
+
+    forward_copy(me, half).start()
+    load_id.wait()
     w_id[...] = log_weight(id_count[...])
+
+    def round_ident(c):
+        rows = ids[:, column(c)].astype(BF16)
+        right[half, c] = rows
+        w_right[c] = (rows.astype(F32) * w_id[pl.ds(c, 1), :]).astype(BF16)
+
+    unrolled(idents, round_ident)
+    right_copy(half).start()
 
     place = lax.broadcasted_iota(jnp.int32, (1, blocks), 1)
     code = ((place * 128 + slot_row[...]) * 32 + id_row[...]).astype(F32)
-    slots = lax.broadcasted_iota(jnp.int32, (1, peers), 1).astype(F32)
     for row, key, payload in (
         (0, slot_row[...].astype(F32), code),
         (2, id_row[...].astype(F32), code),
-        (4, send_row[...].astype(F32), slots),
     ):
         order, last = sorted_codes(key, payload)
         plan[row : row + 1, : order.shape[1]] = order
@@ -102,87 +182,6 @@
     plan_copy = pltpu.make_async_copy(plan, plan_smem, load_sem.at[3])
     plan_copy.start()
 
-    def within(index, count):
-        return jnp.clip(index, 0, count - 1)
-
-    def column(block):
-        return pl.ds(pl.multiple_of(block * blk, blk), blk)
-
-    def unrolled(count, function):
-        @pl.loop(0, count // GROUP)
-        def _(i):
-            for u in range(GROUP):
-                function(i * GROUP + u)
-
-    load_rec.wait()
-
-    def round_record(r):
-        rec_bf[r] = rec[:, column(r)].astype(BF16)
-
-    unrolled(rec_bf.shape[0], round_record)
-
-    @pl.loop(0, peers)
-    def _(peer):
-        wanted = send_list[peer]
-        left_send[peer] = rec_bf[wanted]
-        weight_send[peer] = w_rec[wanted]
-
-    left[half, me] = left_send[me]
-    weight_got[me] = weight_send[me]
-    load_id.wait()
-
-    def round_ident(c):
-        rows = ids[:, column(c)].astype(BF16)
-        right[half, c] = rows
-        w_right[c] = (rows.astype(F32) * w_id[pl.ds(c, 1), :]).astype(BF16)
-
-    unrolled(idents, round_ident)
-    pl.semaphore_wait(barrier, peers)
-
-    def left_copy(peer, slot):
-        return pltpu.make_async_remote_copy(
-            src_ref=left_send.at[peer], dst_ref=left.at[half, slot],
-            send_sem=ls.at[peer], recv_sem=lr.at[slot],
-            device_id={"gx": peer}, device_id_type=MESH,
-        )
-
-    def weight_copy(peer, slot):
-        return pltpu.make_async_remote_copy(
-            src_ref=weight_send.at[peer], dst_ref=weight_got.at[slot],
-            send_sem=ws.at[peer], recv_sem=wr.at[slot],
-            device_id={"gx": peer}, device_id_type=MESH,
-        )
-
-    def forward_copy(slot, side):
-        return pltpu.make_async_remote_copy(
-            src_ref=left.at[side, slot], dst_ref=left.at[side, slot],
-            send_sem=fs.at[slot], recv_sem=fr.at[slot],
-            device_id={"gy": other}, device_id_type=MESH,
-        )
-
-    def back_copy(peer, slot):
-        return pltpu.make_async_remote_copy(
-            src_ref=back.at[peer], dst_ref=ret.at[slot],
-            send_sem=bs.at[peer], recv_sem=br.at[slot],
-            device_id={"gx": peer}, device_id_type=MESH,
-        )
-
-    def right_copy(side):
-        return pltpu.make_async_remote_copy(
-            src_ref=right.at[side], dst_ref=right.at[side],
-            send_sem=rs, recv_sem=rr,
-            device_id={"gy": other}, device_id_type=MESH,
-        )
-
-    right_copy(half).start()
-
-    @pl.loop(1, peers)
-    def _(step):
-        peer = lax.rem(me + step, peers)
-        left_copy(peer, me).start()
-        weight_copy(peer, me).start()
-
-    forward_copy(me, half).start()
 
     right_copy(other).wait_recv()
 
@@ -274,23 +273,8 @@
         source = lax.rem(me - step + peers, peers)
         back_copy(source, source).wait_recv()
 
-    def add_returned(p, acc):
-        code = plan_smem[4, p]
-        acc = acc * (code & 1).astype(F32) + ret[within(code >> 1, peers)].astype(F32)
-        total[p] = acc
-        return acc
-
-    lax.fori_loop(0, peers, add_returned, jnp.zeros(total.shape[1:], F32))
-
-    def finish_record(r):
-        at = within(plan_smem[5, r] >> 1, blocks)
-        used = (plan_smem[5, r] & 1).astype(F32)
-        old = rec[:, column(r)]
-        rec[:, column(r)] = old - RATE * (total[at] * used + DECAY * old)
-
-    unrolled(rec_bf.shape[0], finish_record)
-    store_rec = pltpu.make_async_copy(rec, new_rec_out, load_sem.at[0])
-    store_rec.start()
+    store_ret = pltpu.make_async_copy(ret, ret_out, load_sem.at[0])
+    store_ret.start()
 
     right_copy(half).wait_send()
     forward_copy(me, half).wait_send()
@@ -304,7 +288,7 @@
         back_copy(peer, me).wait_send()
 
     store_id.wait()
-    store_rec.wait()
+    store_ret.wait()
 
 
 def exchange(send_list, slot_of_block, id_of_block, rec_count, id_count, rec_t, id_t, obs):
@@ -314,16 +298,17 @@
     idents = id_count.shape[0]
     smem = pl.BlockSpec(memory_space=pltpu.SMEM)
     vmem = pl.BlockSpec(memory_space=pltpu.VMEM)
-    hbm = pl.BlockSpec(memory_space=pl.ANY)
+    hbm = pl.BlockSpec(memory_space=pltpu.HBM)
+    anywhere = pl.BlockSpec(memory_space=pl.ANY)
     dma = pltpu.SemaphoreType.DMA
     return pl.pallas_call(
         exchange_kernel,
         out_shape=(
-            jax.ShapeDtypeStruct(rec_t.shape, F32),
+            jax.ShapeDtypeStruct((peers, half_cols, blk), BF16),
             jax.ShapeDtypeStruct(id_t.shape, F32),
         ),
-        in_specs=[smem] + [vmem] * 5 + [hbm] * 3,
-        out_specs=(hbm, hbm),
+        in_specs=[smem] + [vmem] * 4 + [hbm] * 3,
+        out_specs=(anywhere, anywhere),
         scratch_shapes=[
             pltpu.VMEM(rec_t.shape, F32),
             pltpu.VMEM((rec_count.shape[0], half_cols, blk), BF16),
@@ -351,27 +336,90 @@
         + [dma((peers,))] * 8
         + [dma, dma],
         compiler_params=pltpu.CompilerParams(
-            collective_id=0, has_side_effects=True, vmem_limit_bytes=56 << 20
+            collective_id=0, has_side_effects=True, vmem_limit_bytes=(32 << 20) + (peers << 17)
         ),
         name="exchange",
     )(
-        send_list, send_list[None], slot_of_block[None], id_of_block[None],
+        send_list, slot_of_block[None], id_of_block[None],
         rec_count, id_count, rec_t, id_t, obs,
     )
 
 
+def update_kernel(send_list, rec_in, ret_in, new_id, new_rec, id_out, rec, ret, sem, parts):
+    blk = ret.shape[2]
+    width = rec.shape[1] // PARTS
+
+    def part(k):
+        return pl.ds(k * width, width)
+
+    def load(k):
+        return pltpu.make_async_copy(rec_in.at[:, part(k)], rec.at[:, part(k)], parts.at[k])
+
+    def store(k):
+        return pltpu.make_async_copy(rec.at[:, part(k)], new_rec.at[:, part(k)], parts.at[k])
+
+    load_ret = pltpu.make_async_copy(ret_in, ret, sem.at[0])
+    pass_on = pltpu.make_async_copy(new_id, id_out, sem.at[1])
+    for k in range(PARTS):
+        load(k).start()
+    load_ret.start()
+    pass_on.start()
+    for k in range(PARTS):
+        load(k).wait()
+    load_ret.wait()
+    shrink = 1.0 - RATE * DECAY
+
+    @pl.loop(0, ret.shape[0])
+    def _(s):
+        cols = pl.ds(pl.multiple_of(send_list[s] * blk, blk), blk)
+        rec[:, cols] = rec[:, cols] - (RATE / shrink) * ret[s].astype(F32)
+
+    for k in range(PARTS):
+        rec[:, part(k)] = rec[:, part(k)] * shrink
+        store(k).start()
+    for k in range(PARTS):
+        store(k).wait()
+    pass_on.wait()
+
+
+def update(send_list, rec_t, ret, new_id):
+    hbm = pl.BlockSpec(memory_space=pltpu.HBM)
+    anywhere = pl.BlockSpec(memory_space=pl.ANY)
+    dma = pltpu.SemaphoreType.DMA
+    return pl.pallas_call(
+        update_kernel,
+        out_shape=(
+            jax.ShapeDtypeStruct(rec_t.shape, F32),
+            jax.ShapeDtypeStruct(new_id.shape, F32),
+        ),
+        in_specs=[pl.BlockSpec(memory_space=pltpu.SMEM)] + [anywhere] * 3,
+        out_specs=(hbm, hbm),
+        scratch_shapes=[
+            pltpu.VMEM(rec_t.shape, F32),
+            pltpu.VMEM(ret.shape, BF16),
+            dma((2,)),
+            dma((PARTS,)),
+        ],
+        compiler_params=pltpu.CompilerParams(vmem_limit_bytes=16 << 20),
+        name="update",
+    )(send_list, rec_t, ret, new_id)
+
+
 def body(records, idents, rec_count, id_count, observed, send_list, slot_of_block, id_of_block):
     blk = observed.shape[1]
-    new_rec, new_id = exchange(
-        send_list.reshape(-1),
+    wanted = send_list.reshape(-1)
+    rec_t = records.T
+    ret, new_id = exchange(
+        wanted,
         slot_of_block,
         id_of_block,
         rec_count.reshape(-1, blk),
         id_count.reshape(-1, blk),
-        records.T,
+        rec_t,
         idents.T,
         observed,
     )
+    new_rec, new_id = update(wanted, rec_t, ret, new_id)
     return new_rec.T, new_id.T
 
 

time: 33 us -> 38.5 us (1.17)
  local copies, waits for them, and re-layouts: 3.73 us -> 8.87 us
    unnamed x4 -> x16, local copies, waits for them, and re-layouts: 3.73 us -> 8.87 us
    pallas_call x1 -> x2, Pallas kernels: 28.4 us -> 28.6 us  [the longest x1 26.4 us: exchange(): pl.pallas_call(exchange_kernel, out_shape=(jax.ShapeDtypeStruct((peers, h...]
where the time goes in v3:
time: 38.5 us; the launch traced here: 38.2 us
  Pallas kernels  28.6 us (74%)
  local copies, waits for them, and re-layouts  8.87 us (23%)
  between operations  0.66 us (2%)
    pallas_call x1, Pallas kernels, exchange(): pl.pallas_call(exchange_kernel, out_shape=(jax.ShapeDtypeStruct((peers, h...  26.4 us
    unnamed x16, local copies, waits for them, and re-layouts  8.87 us
    pallas_call x1, Pallas kernels, update(): pl.pallas_call(update_kernel, out_shape=(jax.ShapeDtypeStruct(rec_t.shape...  2.25 us

profile of v3, /device:TPU:0, one launch (start us, length us, event | category | flops | bytes accessed | tf_op | source)
XLA Modules:
  0.0 38.2 jit_solution(14031100621520495253)
XLA Ops:
  0.6 0.0 copy-start
  0.6 2.8 %copy-done = bf16[192,128,128]{2,1,0:T(8,128)(2,1)S(1)} copy-done((bf16[192,128,128]{2,1,0:T(8,128)(2,1)S(1)}, bf16[192,128,128]{2,1,0:T(8,128)(2,1)}, u32[]{:S(2)}) %copy-start) | copy-done | bytes 6291480
  3.4 0.0 copy-start.1
  3.4 1.4 %copy-done.1 = f32[6144,64]{0,1:T(8,128)S(1)} copy-done((f32[6144,64]{0,1:T(8,128)S(1)}, f32[6144,64]{0,1:T(8,128)}, u32[]{:S(2)}) %copy-start.1) | copy-done | bytes 1572888
  4.8 0.0 copy-start.2
  4.8 1.2 %copy-done.2 = f32[4096,64]{0,1:T(8,128)S(1)} copy-done((f32[4096,64]{0,1:T(8,128)S(1)}, f32[4096,64]{0,1:T(8,128)}, u32[]{:S(2)}) %copy-start.2) | copy-done | bytes 1048600
  6.1 0.0 copy-start.3
  6.1 0.7 %copy-done.3 = s32[6144]{0:T(1024)S(1)} copy-done((s32[6144]{0:T(1024)S(1)}, s32[6144]{0:T(1024)}, u32[]{:S(2)}) %copy-start.3) | copy-done | bytes 24600
  6.8 0.0 copy-start.4
  6.8 0.7 %copy-done.4 = s32[4096]{0:T(1024)S(1)} copy-done((s32[4096]{0:T(1024)S(1)}, s32[4096]{0:T(1024)}, u32[]{:S(2)}) %copy-start.4) | copy-done | bytes 16408
  7.5 0.0 copy-start.5
  7.5 0.7 %copy-done.5 = s32[16,1]{0,1:T(1,128)S(1)} copy-done((s32[16,1]{0,1:T(1,128)S(1)}, s32[16,1]{0,1:T(1,128)}, u32[]{:S(2)}) %copy-start.5) | copy-done | bytes 88
  8.2 0.0 copy-start.6
  8.2 0.7 %copy-done.6 = s32[192]{0:T(256)S(1)} copy-done((s32[192]{0:T(256)S(1)}, s32[192]{0:T(256)}, u32[]{:S(2)}) %copy-start.6) | copy-done | bytes 792
  8.8 0.0 copy-start.7
  8.8 0.7 %copy-done.7 = s32[192]{0:T(256)S(1)} copy-done((s32[192]{0:T(256)S(1)}, s32[192]{0:T(256)}, u32[]{:S(2)}) %copy-start.7) | copy-done | bytes 792
  9.5 26.4 %exchange.1 = (bf16[16,64,128]{2,1,0:T(8,128)(2,1)S(1)}, f32[64,4096]{1,0:T(8,128)S(1)}) custom-call(s32[16]{0:T(128)S(1)} %bitcast.14, s32[1,192]{1,0:T(1,128)S(1)} %bitcast.16, s32[1,192]{1,0:T(1,128)S(1)} %bitcast.17, s32[48,128]{1,0:T(8,128)S(1)} %bitcast.12, s32[32,128]{1,0:T(8,128)S(1)} %bitcast.13, f32[64,6144]{1,0:T(8,128)S(1)} %bitcast.9, ...), custom_call_target="tpu_custom_call" | custom-call | tf_op jit(solution)/shard_map/exchange/pallas_call | solution.py:304
  35.9 2.3 %update.1 = (f32[64,6144]{1,0:T(8,128)}, f32[64,4096]{1,0:T(8,128)}) custom-call(s32[16]{0:T(128)S(1)} %bitcast.15, f32[64,6144]{1,0:T(8,128)S(1)} %bitcast.10, bf16[16,64,128]{2,1,0:T(8,128)(2,1)S(1)} %get-tuple-element.6.ret_in, f32[64,4096]{1,0:T(8,128)S(1)} %get-tuple-element.7.new_id), custom_call_target="tpu_custom_call" | custom-call | tf_op jit(solution)/shard_map/update/pallas_call | solution.py:389
Async XLA Ops:
  0.6 2.8 %copy-start = (bf16[192,128,128]{2,1,0:T(8,128)(2,1)S(1)}, bf16[192,128,128]{2,1,0:T(8,128)(2,1)}, u32[]{:S(2)}) copy-start(bf16[192,128,128]{2,1,0:T(8,128)(2,1)} %obs_hbm.1) | copy-start | bytes 18874372
  3.4 1.4 %copy-start.1 = (f32[6144,64]{0,1:T(8,128)S(1)}, f32[6144,64]{0,1:T(8,128)}, u32[]{:S(2)}) copy-start(f32[6144,64]{0,1:T(8,128)} %param.8) | copy-start | bytes 4718596
  4.8 1.2 %copy-start.2 = (f32[4096,64]{0,1:T(8,128)S(1)}, f32[4096,64]{0,1:T(8,128)}, u32[]{:S(2)}) copy-start(f32[4096,64]{0,1:T(8,128)} %param.9) | copy-start | bytes 3145732
  6.1 0.7 %copy-start.3 = (s32[6144]{0:T(1024)S(1)}, s32[6144]{0:T(1024)}, u32[]{:S(2)}) copy-start(s32[6144]{0:T(1024)} %param.10) | copy-start | bytes 73732
  6.8 0.7 %copy-start.4 = (s32[4096]{0:T(1024)S(1)}, s32[4096]{0:T(1024)}, u32[]{:S(2)}) copy-start(s32[4096]{0:T(1024)} %param.11) | copy-start | bytes 49156
  7.5 0.7 %copy-start.5 = (s32[16,1]{0,1:T(1,128)S(1)}, s32[16,1]{0,1:T(1,128)}, u32[]{:S(2)}) copy-start(s32[16,1]{0,1:T(1,128)} %param.13) | copy-start | bytes 196
  8.2 0.7 %copy-start.6 = (s32[192]{0:T(256)S(1)}, s32[192]{0:T(256)}, u32[]{:S(2)}) copy-start(s32[192]{0:T(256)} %param.14) | copy-start | bytes 2308
  8.8 0.7 %copy-start.7 = (s32[192]{0:T(256)S(1)}, s32[192]{0:T(256)}, u32[]{:S(2)}) copy-start(s32[192]{0:T(256)} %param.15) | copy-start | bytes 2308

commit v4 on v3

--- a/solution.py
+++ b/solution.py
@@ -11,6 +11,7 @@
 UNROLL = 16
 GROUP = 4
 PARTS = 4
+VMEM_BYTES = 58 << 20
 LANES = 256
 F32 = jnp.float32
 BF16 = jnp.bfloat16
@@ -336,7 +337,7 @@
         + [dma((peers,))] * 8
         + [dma, dma],
         compiler_params=pltpu.CompilerParams(
-            collective_id=0, has_side_effects=True, vmem_limit_bytes=(32 << 20) + (peers << 17)
+            collective_id=0, has_side_effects=True, vmem_limit_bytes=VMEM_BYTES
         ),
         name="exchange",
     )(
@@ -400,7 +401,7 @@
             dma((2,)),
             dma((PARTS,)),
         ],
-        compiler_params=pltpu.CompilerParams(vmem_limit_bytes=16 << 20),
+        compiler_params=pltpu.CompilerParams(vmem_limit_bytes=VMEM_BYTES),
         name="update",
     )(send_list, rec_t, ret, new_id)
 

time: 38.5 us -> 61.9 us (1.61)
  Pallas kernels: 28.6 us -> 61 us
  local copies, waits for them, and re-layouts: 8.87 us -> 0 us
    pallas_call x1, Pallas kernels: 2.25 us -> 33.6 us  [update(): pl.pallas_call(update_kernel, out_shape=(jax.ShapeDtypeStruct(rec_t.shape...]
    unnamed x16 -> x0, local copies, waits for them, and re-layouts: 8.87 us -> none
    pallas_call x1, Pallas kernels: 26.4 us -> 27.4 us  [exchange(): pl.pallas_call(exchange_kernel, out_shape=(jax.ShapeDtypeStruct((peers, h...]
where the time goes in v4:
time: 61.9 us; the launch traced here: 61.6 us
  Pallas kernels  61 us (99%)
  between operations  0.64 us (1%)
    pallas_call x1, Pallas kernels, update(): pl.pallas_call(update_kernel, out_shape=(jax.ShapeDtypeStruct(rec_t.shape...  33.6 us
    pallas_call x1, Pallas kernels, exchange(): pl.pallas_call(exchange_kernel, out_shape=(jax.ShapeDtypeStruct((peers, h...  27.4 us

profile of v4, /device:TPU:0, one launch (start us, length us, event | category | flops | bytes accessed | tf_op | source)
XLA Modules:
  0.0 61.6 jit_solution(17782155366316010232)
XLA Ops:
  0.6 27.4 %exchange.1 = (bf16[16,64,128]{2,1,0:T(8,128)(2,1)}, f32[64,4096]{1,0:T(8,128)}) custom-call(s32[16]{0:T(128)} %bitcast.14, s32[1,192]{1,0:T(1,128)} %bitcast.16, s32[1,192]{1,0:T(1,128)} %bitcast.17, s32[48,128]{1,0:T(8,128)} %bitcast.12, s32[32,128]{1,0:T(8,128)} %bitcast.13, f32[64,6144]{1,0:T(8,128)} %bitcast.9, f32[64,4096]{1,0:T(8,128)} %bitcast.11, ...), custom_call_target="tpu_custom_call" | custom-call | tf_op jit(solution)/shard_map/exchange/pallas_call | solution.py:305
  28.0 33.6 %update.1 = (f32[64,6144]{1,0:T(8,128)}, f32[64,4096]{1,0:T(8,128)}) custom-call(s32[16]{0:T(128)} %bitcast.15, f32[64,6144]{1,0:T(8,128)} %bitcast.10, bf16[16,64,128]{2,1,0:T(8,128)(2,1)} %get-tuple-element.6.ret_in, f32[64,4096]{1,0:T(8,128)} %get-tuple-element.7.new_id), custom_call_target="tpu_custom_call" | custom-call | tf_op jit(solution)/shard_map/update/pallas_call | solution.py:390

commit v5 on v4

--- a/solution.py
+++ b/solution.py
@@ -8,11 +8,10 @@
 MESH = pl.DeviceIdType.MESH
 RATE = 0.05
 DECAY = 0.1
-UNROLL = 16
+UNROLL = 8
 GROUP = 4
 PARTS = 4
 VMEM_BYTES = 58 << 20
-LANES = 256
 F32 = jnp.float32
 BF16 = jnp.bfloat16
 
@@ -27,6 +26,10 @@
 
 def log_weight(count):
     return jnp.log(1.0 + count.astype(F32)) / jnp.log(F32(1001.0))
+
+
+def pairs_for(blocks, keys):
+    return -(-(blocks + keys) // (2 * UNROLL)) * UNROLL
 
 
 def column_of(row):
@@ -37,19 +40,29 @@
     return jnp.sum(jnp.where(diagonal, row, 0.0), axis=1, keepdims=True)
 
 
-def sorted_codes(key, payload):
+def sorted_codes(key, payload, lanes):
     size = key.shape[1]
     across = lax.broadcasted_iota(jnp.int32, (size, size), 1)
-    ahead = across < lax.broadcasted_iota(jnp.int32, (size, size), 0)
+    down = lax.broadcasted_iota(jnp.int32, (size, size), 0)
     key_col = column_of(key)
-    earlier = jnp.sum(jnp.where((key == key_col) & ahead, 1.0, 0.0), axis=1, keepdims=True)
-    rank = earlier + jnp.sum(jnp.where(key < key_col, 1.0, 0.0), axis=1, keepdims=True)
+    equal = jnp.where(key == key_col, 1.0, 0.0)
+
+    def places(count, earlier):
+        odd = count - 2.0 * jnp.floor(0.5 * count)
+        return 1.0 + jnp.where(earlier == 0.0, odd, 0.0)
+
+    earlier = jnp.sum(jnp.where(across < down, equal, 0.0), axis=1, keepdims=True)
+    places_col = places(jnp.sum(equal, axis=1, keepdims=True), earlier)
+    earlier_row = jnp.sum(jnp.where(down < across, equal, 0.0), axis=0, keepdims=True)
+    places_row = places(jnp.sum(equal, axis=0, keepdims=True), earlier_row)
+    smaller = jnp.where(key < key_col, places_row, 0.0)
+    rank = earlier + jnp.sum(smaller, axis=1, keepdims=True)
     marked = 2.0 * column_of(payload) + jnp.minimum(earlier, 1.0)
-    order = jnp.sum(jnp.where(rank == across.astype(F32), marked, 0.0), axis=0, keepdims=True)
-    value = lax.broadcasted_iota(jnp.int32, (1, LANES), 1).astype(F32)
-    up_to = jnp.sum(jnp.where(key_col <= value, 1.0, 0.0), axis=0, keepdims=True)
+    value = lax.broadcasted_iota(jnp.int32, (1, lanes), 1).astype(F32)
+    order = jnp.sum(jnp.where(rank == value, marked, 0.0), axis=0, keepdims=True)
+    up_to = jnp.sum(jnp.where(key_col <= value, places_col, 0.0), axis=0, keepdims=True)
     used = jnp.sum(jnp.where(key_col == value, 1.0, 0.0), axis=0, keepdims=True)
-    last = 2.0 * jnp.maximum(up_to - 1.0, 0.0) + jnp.minimum(used, 1.0)
+    last = 2.0 * jnp.maximum(0.5 * up_to - 1.0, 0.0) + jnp.minimum(used, 1.0)
     return order.astype(jnp.int32), last.astype(jnp.int32)
 
 
@@ -65,7 +78,7 @@
     me = lax.axis_index("gx")
     half = lax.axis_index("gy")
     other = 1 - half
-    idents = w_right.shape[0]
+    idents = id_count.shape[0]
     blocks = obs.shape[0]
     blk = obs.shape[1]
 
@@ -100,6 +113,18 @@
             for u in range(GROUP):
                 function(i * GROUP + u)
 
+    place = lax.broadcasted_iota(jnp.int32, (1, blocks), 1)
+    code = ((place * 256 + slot_row[...] + 1) * 64 + id_row[...] + 1).astype(F32)
+    for row, key in ((0, slot_row), (2, id_row)):
+        order, last = sorted_codes(key[...].astype(F32), code, plan.shape[1])
+        plan[row : row + 1, :] = order
+        plan[row + 1 : row + 2, :] = last
+    plan_copy = pltpu.make_async_copy(plan, plan_smem, load_sem.at[3])
+    plan_copy.start()
+    w_right[0] = jnp.zeros(w_right.shape[1:], BF16)
+    w_left[0] = jnp.zeros(w_left.shape[1:], BF16)
+    gram[0] = jnp.zeros(gram.shape[1:], F32)
+
     load_rec.wait()
     load_obs.start()
 
@@ -166,24 +191,11 @@
     def round_ident(c):
         rows = ids[:, column(c)].astype(BF16)
         right[half, c] = rows
-        w_right[c] = (rows.astype(F32) * w_id[pl.ds(c, 1), :]).astype(BF16)
+        w_right[c + 1] = (rows.astype(F32) * w_id[pl.ds(c, 1), :]).astype(BF16)
 
     unrolled(idents, round_ident)
     right_copy(half).start()
 
-    place = lax.broadcasted_iota(jnp.int32, (1, blocks), 1)
-    code = ((place * 128 + slot_row[...]) * 32 + id_row[...]).astype(F32)
-    for row, key, payload in (
-        (0, slot_row[...].astype(F32), code),
-        (2, id_row[...].astype(F32), code),
-    ):
-        order, last = sorted_codes(key, payload)
-        plan[row : row + 1, : order.shape[1]] = order
-        plan[row + 1 : row + 2, :] = last
-    plan_copy = pltpu.make_async_copy(plan, plan_smem, load_sem.at[3])
-    plan_copy.start()
-
-
     right_copy(other).wait_recv()
 
     def full_right(c):
@@ -193,22 +205,25 @@
         return jnp.concatenate([left[0, s], left[1, s]], axis=0)
 
     def right_gram(c):
-        gram[c] = dot_nt(w_right[c], full_right(c))
+        gram[c + 1] = dot_nt(w_right[c + 1], full_right(c))
 
     unrolled(idents, right_gram)
     load_obs.wait()
     plan_copy.wait()
 
-    def running_sums(row, term):
+    def running_sums(row, pairs, term):
+        def one(place):
+            code = plan_smem[row, place]
+            return within(code >> 15, blocks), within((code >> 7) & 255, peers + 1), within(
+                (code >> 1) & 63, idents + 1
+            )
+
         def step(i, carry):
             acc, acc_gram = carry
             for u in range(UNROLL):
                 p = i * UNROLL + u
-                code = plan_smem[row, p]
-                keep = (code & 1).astype(F32)
-                product, matrix = term(
-                    within(code >> 13, blocks), within((code >> 6) & 127, peers), (code >> 1) & 31
-                )
+                keep = (plan_smem[row, 2 * p] & 1).astype(F32)
+                product, matrix = term(one(2 * p), one(2 * p + 1))
                 acc = acc * keep + product
                 acc_gram = acc_gram * keep + matrix
                 total[p] = acc
@@ -216,19 +231,31 @@
             return acc, acc_gram
 
         zero = jnp.zeros(total.shape[1:], F32)
-        lax.fori_loop(0, blocks // UNROLL, step, (zero, zero))
-
-    running_sums(0, lambda b, s, c: (dot_nt(w_right[c], obs[b]), gram[c]))
+        lax.fori_loop(0, pairs // UNROLL, step, (zero, zero))
+
+    def slot_term(first, second):
+        (b0, _, c0), (b1, _, c1) = first, second
+        factors = jnp.concatenate([w_right[c0], w_right[c1]], axis=1)
+        values = jnp.concatenate([obs[b0], obs[b1]], axis=1)
+        return dot_nt(factors, values), gram[c0] + gram[c1]
+
+    def id_term(first, second):
+        (b0, s0, _), (b1, s1, _) = first, second
+        factors = jnp.concatenate([w_left[s0], w_left[s1]], axis=1)
+        values = jnp.concatenate([obs[b0], obs[b1]], axis=0)
+        return dot_nn(factors, values), gram[s0] + gram[s1]
+
+    running_sums(0, pairs_for(blocks, peers), slot_term)
 
     def finish_slot(s):
-        last = within(plan_smem[1, s] >> 1, blocks)
+        last = within(plan_smem[1, s] >> 1, total.shape[0])
         score = dot_nn(total_gram[last].astype(BF16), full_left(s))
         back[s] = ((score - total[last]) * weight_got[s]).astype(BF16)
 
     def left_factors(s):
         rows = (left[half, s].astype(F32) * weight_got[s]).astype(BF16)
-        w_left[s] = rows
-        gram[s] = dot_nt(rows, full_left(s))
+        w_left[s + 1] = rows
+        gram[s + 1] = dot_nt(rows, full_left(s))
 
     @pl.loop(1, peers)
     def _(step):
@@ -255,10 +282,10 @@
 
     ret[me] = back[me]
     unrolled(peers, left_factors)
-    running_sums(2, lambda b, s, c: (dot_nn(w_left[s], obs[b]), gram[s]))
+    running_sums(2, pairs_for(blocks, idents), id_term)
 
     def finish_ident(c):
-        at = within(plan_smem[3, c] >> 1, blocks)
+        at = within(plan_smem[3, c] >> 1, total.shape[0])
         used = (plan_smem[3, c] & 1).astype(F32)
         score = dot_nn(total_gram[at].astype(BF16), full_right(c))
         grad = (score - total[at]) * (w_id[pl.ds(c, 1), :] * used)
@@ -297,6 +324,8 @@
     half_cols = rec_t.shape[0]
     blocks, blk, _ = obs.shape
     idents = id_count.shape[0]
+    pairs = pairs_for(blocks, max(peers, idents))
+    lanes = -(-2 * pairs // 128) * 128
     smem = pl.BlockSpec(memory_space=pltpu.SMEM)
     vmem = pl.BlockSpec(memory_space=pltpu.VMEM)
     hbm = pl.BlockSpec(memory_space=pltpu.HBM)
@@ -320,18 +349,18 @@
             pltpu.VMEM(id_count.shape, F32),
             pltpu.VMEM((2, peers, half_cols, blk), BF16),
             pltpu.VMEM((2, idents, half_cols, blk), BF16),
-            pltpu.VMEM((idents, half_cols, blk), BF16),
-            pltpu.VMEM((peers, half_cols, blk), BF16),
-            pltpu.VMEM((max(idents, peers), half_cols, 2 * half_cols), F32),
+            pltpu.VMEM((idents + 1, half_cols, blk), BF16),
+            pltpu.VMEM((peers + 1, half_cols, blk), BF16),
+            pltpu.VMEM((max(idents, peers) + 1, half_cols, 2 * half_cols), F32),
             pltpu.VMEM((peers, half_cols, blk), BF16),
             pltpu.VMEM((peers, 1, blk), F32),
             pltpu.VMEM((peers, 1, blk), F32),
             pltpu.VMEM((peers, half_cols, blk), BF16),
             pltpu.VMEM((peers, half_cols, blk), BF16),
-            pltpu.VMEM((blocks, half_cols, blk), F32),
-            pltpu.VMEM((blocks, half_cols, 2 * half_cols), F32),
-            pltpu.VMEM((8, LANES), jnp.int32),
-            pltpu.SMEM((8, LANES), jnp.int32),
+            pltpu.VMEM((pairs, half_cols, blk), F32),
+            pltpu.VMEM((pairs, half_cols, 2 * half_cols), F32),
+            pltpu.VMEM((8, lanes), jnp.int32),
+            pltpu.SMEM((8, lanes), jnp.int32),
             dma((4,)),
         ]
         + [dma((peers,))] * 8
@@ -346,7 +375,9 @@
     )
 
 
-def update_kernel(send_list, rec_in, ret_in, new_id, new_rec, id_out, rec, ret, sem, parts):
+def update_kernel(
+    send_list, rec_in, ret_in, new_id, new_rec, id_out, rec, ret, ids, sem, parts
+):
     blk = ret.shape[2]
     width = rec.shape[1] // PARTS
 
@@ -360,14 +391,17 @@
         return pltpu.make_async_copy(rec.at[:, part(k)], new_rec.at[:, part(k)], parts.at[k])
 
     load_ret = pltpu.make_async_copy(ret_in, ret, sem.at[0])
-    pass_on = pltpu.make_async_copy(new_id, id_out, sem.at[1])
+    load_id = pltpu.make_async_copy(new_id, ids, sem.at[1])
+    store_id = pltpu.make_async_copy(ids, id_out, sem.at[1])
     for k in range(PARTS):
         load(k).start()
     load_ret.start()
-    pass_on.start()
+    load_id.start()
     for k in range(PARTS):
         load(k).wait()
     load_ret.wait()
+    load_id.wait()
+    store_id.start()
     shrink = 1.0 - RATE * DECAY
 
     @pl.loop(0, ret.shape[0])
@@ -380,7 +414,7 @@
         store(k).start()
     for k in range(PARTS):
         store(k).wait()
-    pass_on.wait()
+    store_id.wait()
 
 
 def update(send_list, rec_t, ret, new_id):
@@ -398,6 +432,7 @@
         scratch_shapes=[
             pltpu.VMEM(rec_t.shape, F32),
             pltpu.VMEM(ret.shape, BF16),
+            pltpu.VMEM(new_id.shape, F32),
             dma((2,)),
             dma((PARTS,)),
         ],

time: 61.9 us -> 31.1 us (0.50)
  Pallas kernels: 61 us -> 30.2 us
    pallas_call x1, Pallas kernels: 33.6 us -> 3.98 us  [update(): pl.pallas_call(update_kernel, out_shape=(jax.ShapeDtypeStruct(rec_t.shape...]
    pallas_call x1, Pallas kernels: 27.4 us -> 26.2 us  [exchange(): pl.pallas_call(exchange_kernel, out_shape=(jax.ShapeDtypeStruct((peers, h...]
where the time goes in v5:
time: 31.1 us; the launch traced here: 30.8 us
  Pallas kernels  30.2 us (97%)
  between operations  0.64 us (2%)
    pallas_call x1, Pallas kernels, exchange(): pl.pallas_call(exchange_kernel, out_shape=(jax.ShapeDtypeStruct((peers, h...  26.2 us
    pallas_call x1, Pallas kernels, update(): pl.pallas_call(update_kernel, out_shape=(jax.ShapeDtypeStruct(rec_t.shape...  3.98 us

profile of v5, /device:TPU:0, one launch (start us, length us, event | category | flops | bytes accessed | tf_op | source)
XLA Modules:
  0.0 30.8 jit_solution(11429627729482451682)
XLA Ops:
  0.6 26.2 %exchange.1 = (bf16[16,64,128]{2,1,0:T(8,128)(2,1)}, f32[64,4096]{1,0:T(8,128)}) custom-call(s32[16]{0:T(128)} %bitcast.14, s32[1,192]{1,0:T(1,128)} %bitcast.16, s32[1,192]{1,0:T(1,128)} %bitcast.17, s32[48,128]{1,0:T(8,128)} %bitcast.12, s32[32,128]{1,0:T(8,128)} %bitcast.13, f32[64,6144]{1,0:T(8,128)} %bitcast.9, f32[64,4096]{1,0:T(8,128)} %bitcast.11, ...), custom_call_target="tpu_custom_call" | custom-call | tf_op jit(solution)/shard_map/exchange/pallas_call | solution.py:334
  26.8 4.0 %update.1 = (f32[64,6144]{1,0:T(8,128)}, f32[64,4096]{1,0:T(8,128)}) custom-call(s32[16]{0:T(128)} %bitcast.15, f32[64,6144]{1,0:T(8,128)} %bitcast.10, bf16[16,64,128]{2,1,0:T(8,128)(2,1)} %get-tuple-element.6.ret_in, f32[64,4096]{1,0:T(8,128)} %get-tuple-element.7.new_id), custom_call_target="tpu_custom_call" | custom-call | tf_op jit(solution)/shard_map/update/pallas_call | solution.py:424

commit v6 on v5

--- a/solution.py
+++ b/solution.py
@@ -113,18 +113,6 @@
             for u in range(GROUP):
                 function(i * GROUP + u)
 
-    place = lax.broadcasted_iota(jnp.int32, (1, blocks), 1)
-    code = ((place * 256 + slot_row[...] + 1) * 64 + id_row[...] + 1).astype(F32)
-    for row, key in ((0, slot_row), (2, id_row)):
-        order, last = sorted_codes(key[...].astype(F32), code, plan.shape[1])
-        plan[row : row + 1, :] = order
-        plan[row + 1 : row + 2, :] = last
-    plan_copy = pltpu.make_async_copy(plan, plan_smem, load_sem.at[3])
-    plan_copy.start()
-    w_right[0] = jnp.zeros(w_right.shape[1:], BF16)
-    w_left[0] = jnp.zeros(w_left.shape[1:], BF16)
-    gram[0] = jnp.zeros(gram.shape[1:], F32)
-
     load_rec.wait()
     load_obs.start()
 
@@ -196,7 +184,21 @@
     unrolled(idents, round_ident)
     right_copy(half).start()
 
-    right_copy(other).wait_recv()
+    place = lax.broadcasted_iota(jnp.int32, (1, blocks), 1)
+    code = ((place * 256 + slot_row[...] + 1) * 64 + id_row[...] + 1).astype(F32)
+
+    def sort_by(which, key):
+        order, last = sorted_codes(key[...].astype(F32), code, plan.shape[2])
+        plan[which, 0:1, :] = order
+        plan[which, 1:2, :] = last
+        copy = pltpu.make_async_copy(plan.at[which], plan_smem.at[which], load_sem.at[3 + which])
+        copy.start()
+        return copy
+
+    slot_plan = sort_by(0, slot_row)
+    w_right[0] = jnp.zeros(w_right.shape[1:], BF16)
+    w_left[0] = jnp.zeros(w_left.shape[1:], BF16)
+    gram[0] = jnp.zeros(gram.shape[1:], F32)
 
     def full_right(c):
         return jnp.concatenate([right[0, c], right[1, c]], axis=0)
@@ -207,55 +209,47 @@
     def right_gram(c):
         gram[c + 1] = dot_nt(w_right[c + 1], full_right(c))
 
-    unrolled(idents, right_gram)
-    load_obs.wait()
-    plan_copy.wait()
-
-    def running_sums(row, pairs, term):
+
+    def running_sums(which, pairs, terms, sums):
         def one(place):
-            code = plan_smem[row, place]
+            code = plan_smem[which, 0, place]
             return within(code >> 15, blocks), within((code >> 7) & 255, peers + 1), within(
                 (code >> 1) & 63, idents + 1
             )
 
         def step(i, carry):
-            acc, acc_gram = carry
             for u in range(UNROLL):
                 p = i * UNROLL + u
-                keep = (plan_smem[row, 2 * p] & 1).astype(F32)
-                product, matrix = term(one(2 * p), one(2 * p + 1))
-                acc = acc * keep + product
-                acc_gram = acc_gram * keep + matrix
-                total[p] = acc
-                total_gram[p] = acc_gram
-            return acc, acc_gram
-
-        zero = jnp.zeros(total.shape[1:], F32)
-        lax.fori_loop(0, pairs // UNROLL, step, (zero, zero))
-
-    def slot_term(first, second):
+                keep = (plan_smem[which, 0, 2 * p] & 1).astype(F32)
+                new = terms(one(2 * p), one(2 * p + 1))
+                carry = tuple(acc * keep + term for acc, term in zip(carry, new))
+                for ref, acc in zip(sums, carry):
+                    ref[p] = acc
+            return carry
+
+        zero = tuple(jnp.zeros(ref.shape[1:], F32) for ref in sums)
+        lax.fori_loop(0, pairs // UNROLL, step, zero)
+
+    def slot_product(first, second):
         (b0, _, c0), (b1, _, c1) = first, second
         factors = jnp.concatenate([w_right[c0], w_right[c1]], axis=1)
         values = jnp.concatenate([obs[b0], obs[b1]], axis=1)
-        return dot_nt(factors, values), gram[c0] + gram[c1]
-
-    def id_term(first, second):
+        return (dot_nt(factors, values),)
+
+    def slot_gram(first, second):
+        return (gram[first[2]] + gram[second[2]],)
+
+    def id_terms(first, second):
         (b0, s0, _), (b1, s1, _) = first, second
         factors = jnp.concatenate([w_left[s0], w_left[s1]], axis=1)
         values = jnp.concatenate([obs[b0], obs[b1]], axis=0)
         return dot_nn(factors, values), gram[s0] + gram[s1]
 
-    running_sums(0, pairs_for(blocks, peers), slot_term)
-
-    def finish_slot(s):
-        last = within(plan_smem[1, s] >> 1, total.shape[0])
-        score = dot_nn(total_gram[last].astype(BF16), full_left(s))
-        back[s] = ((score - total[last]) * weight_got[s]).astype(BF16)
-
-    def left_factors(s):
-        rows = (left[half, s].astype(F32) * weight_got[s]).astype(BF16)
-        w_left[s + 1] = rows
-        gram[s + 1] = dot_nt(rows, full_left(s))
+    slot_plan.wait()
+    load_obs.wait()
+    running_sums(0, pairs_for(blocks, peers), slot_product, (total,))
+    right_copy(other).wait_recv()
+    unrolled(idents, right_gram)
 
     @pl.loop(1, peers)
     def _(step):
@@ -263,6 +257,18 @@
         left_copy(source, source).wait_recv()
         weight_copy(source, source).wait_recv()
         forward_copy(source, half).start()
+
+    running_sums(0, pairs_for(blocks, peers), slot_gram, (total_gram,))
+
+    def finish_slot(s):
+        last = within(plan_smem[0, 1, s] >> 1, total.shape[0])
+        score = dot_nn(total_gram[last].astype(BF16), full_left(s))
+        back[s] = ((score - total[last]) * weight_got[s]).astype(BF16)
+
+    def left_factors(s):
+        rows = (left[half, s].astype(F32) * weight_got[s]).astype(BF16)
+        w_left[s + 1] = rows
+        gram[s + 1] = dot_nt(rows, full_left(s))
 
     @pl.loop(0, peers // GROUP)
     def _(i):
@@ -280,13 +286,15 @@
                 def _():
                     back_copy(source, me).start()
 
+    id_plan = sort_by(1, id_row)
     ret[me] = back[me]
     unrolled(peers, left_factors)
-    running_sums(2, pairs_for(blocks, idents), id_term)
+    id_plan.wait()
+    running_sums(1, pairs_for(blocks, idents), id_terms, (total, total_gram))
 
     def finish_ident(c):
-        at = within(plan_smem[3, c] >> 1, total.shape[0])
-        used = (plan_smem[3, c] & 1).astype(F32)
+        at = within(plan_smem[1, 1, c] >> 1, total.shape[0])
+        used = (plan_smem[1, 1, c] & 1).astype(F32)
         score = dot_nn(total_gram[at].astype(BF16), full_right(c))
         grad = (score - total[at]) * (w_id[pl.ds(c, 1), :] * used)
         old = ids[:, column(c)]
@@ -359,9 +367,9 @@
             pltpu.VMEM((peers, half_cols, blk), BF16),
             pltpu.VMEM((pairs, half_cols, blk), F32),
             pltpu.VMEM((pairs, half_cols, 2 * half_cols), F32),
-            pltpu.VMEM((8, lanes), jnp.int32),
-            pltpu.SMEM((8, lanes), jnp.int32),
-            dma((4,)),
+            pltpu.VMEM((2, 8, lanes), jnp.int32),
+            pltpu.SMEM((2, 8, lanes), jnp.int32),
+            dma((5,)),
         ]
         + [dma((peers,))] * 8
         + [dma, dma],
@@ -397,21 +405,21 @@
         load(k).start()
     load_ret.start()
     load_id.start()
+    shrink = 1.0 - RATE * DECAY
     for k in range(PARTS):
         load(k).wait()
+        rec[:, part(k)] = rec[:, part(k)] * shrink
     load_ret.wait()
-    load_id.wait()
-    store_id.start()
-    shrink = 1.0 - RATE * DECAY
 
     @pl.loop(0, ret.shape[0])
     def _(s):
         cols = pl.ds(pl.multiple_of(send_list[s] * blk, blk), blk)
-        rec[:, cols] = rec[:, cols] - (RATE / shrink) * ret[s].astype(F32)
+        rec[:, cols] = rec[:, cols] - RATE * ret[s].astype(F32)
 
     for k in range(PARTS):
-        rec[:, part(k)] = rec[:, part(k)] * shrink
         store(k).start()
+    load_id.wait()
+    store_id.start()
     for k in range(PARTS):
         store(k).wait()
     store_id.wait()

time: 31.1 us -> 31.3 us (level)
    pallas_call x1, Pallas kernels: 26.2 us -> 26.6 us  [exchange(): pl.pallas_call(exchange_kernel, out_shape=(jax.ShapeDtypeStruct((peers, h...]
where the time goes in v6:
time: 31.3 us; the launch traced here: 31.1 us
  Pallas kernels  30.4 us (97%)
  between operations  0.64 us (2%)
    pallas_call x1, Pallas kernels, exchange(): pl.pallas_call(exchange_kernel, out_shape=(jax.ShapeDtypeStruct((peers, h...  26.6 us
    pallas_call x1, Pallas kernels, update(): pl.pallas_call(update_kernel, out_shape=(jax.ShapeDtypeStruct(rec_t.shape...  3.85 us

profile of v6, /device:TPU:0, one launch (start us, length us, event | category | flops | bytes accessed | tf_op | source)
XLA Modules:
  0.0 31.1 jit_solution(17087646460638600057)
XLA Ops:
  0.6 26.6 %exchange.1 = (bf16[16,64,128]{2,1,0:T(8,128)(2,1)}, f32[64,4096]{1,0:T(8,128)}) custom-call(s32[16]{0:T(128)} %bitcast.14, s32[1,192]{1,0:T(1,128)} %bitcast.16, s32[1,192]{1,0:T(1,128)} %bitcast.17, s32[48,128]{1,0:T(8,128)} %bitcast.12, s32[32,128]{1,0:T(8,128)} %bitcast.13, f32[64,6144]{1,0:T(8,128)} %bitcast.9, f32[64,4096]{1,0:T(8,128)} %bitcast.11, ...), custom_call_target="tpu_custom_call" | custom-call | tf_op jit(solution)/shard_map/exchange/pallas_call | solution.py:342
  27.2 3.8 %update.1 = (f32[64,6144]{1,0:T(8,128)}, f32[64,4096]{1,0:T(8,128)}) custom-call(s32[16]{0:T(128)} %bitcast.15, f32[64,6144]{1,0:T(8,128)} %bitcast.10, bf16[16,64,128]{2,1,0:T(8,128)(2,1)} %get-tuple-element.6.ret_in, f32[64,4096]{1,0:T(8,128)} %get-tuple-element.7.new_id), custom_call_target="tpu_custom_call" | custom-call | tf_op jit(solution)/shard_map/update/pallas_call | solution.py:432

commit v7 on v6

--- a/solution.py
+++ b/solution.py
@@ -9,7 +9,8 @@
 RATE = 0.05
 DECAY = 0.1
 UNROLL = 8
-GROUP = 4
+GROUP = 8
+ROUNDS = 4
 PARTS = 4
 VMEM_BYTES = 58 << 20
 F32 = jnp.float32
@@ -218,8 +219,8 @@
             )
 
         def step(i, carry):
-            for u in range(UNROLL):
-                p = i * UNROLL + u
+            for u in range(width):
+                p = i * width + u
                 keep = (plan_smem[which, 0, 2 * p] & 1).astype(F32)
                 new = terms(one(2 * p), one(2 * p + 1))
                 carry = tuple(acc * keep + term for acc, term in zip(carry, new))
@@ -227,8 +228,9 @@
                     ref[p] = acc
             return carry
 
+        width = pairs // ROUNDS
         zero = tuple(jnp.zeros(ref.shape[1:], F32) for ref in sums)
-        lax.fori_loop(0, pairs // UNROLL, step, zero)
+        lax.fori_loop(0, ROUNDS, step, zero)
 
     def slot_product(first, second):
         (b0, _, c0), (b1, _, c1) = first, second

time: 31.3 us -> 31.4 us (level)
  no operation moved by 1% of the time
where the time goes in v7:
time: 31.4 us; the launch traced here: 31.1 us
  Pallas kernels  30.5 us (97%)
  between operations  0.64 us (2%)
    pallas_call x1, Pallas kernels, exchange(): pl.pallas_call(exchange_kernel, out_shape=(jax.ShapeDtypeStruct((peers, h...  26.6 us
    pallas_call x1, Pallas kernels, update(): pl.pallas_call(update_kernel, out_shape=(jax.ShapeDtypeStruct(rec_t.shape...  3.85 us

profile of v7, /device:TPU:0, one launch (start us, length us, event | category | flops | bytes accessed | tf_op | source)
XLA Modules:
  0.0 31.1 jit_solution(11623302129635823080)
XLA Ops:
  0.6 26.6 %exchange.1 = (bf16[16,64,128]{2,1,0:T(8,128)(2,1)}, f32[64,4096]{1,0:T(8,128)}) custom-call(s32[16]{0:T(128)} %bitcast.14, s32[1,192]{1,0:T(1,128)} %bitcast.16, s32[1,192]{1,0:T(1,128)} %bitcast.17, s32[48,128]{1,0:T(8,128)} %bitcast.12, s32[32,128]{1,0:T(8,128)} %bitcast.13, f32[64,6144]{1,0:T(8,128)} %bitcast.9, f32[64,4096]{1,0:T(8,128)} %bitcast.11, ...), custom_call_target="tpu_custom_call" | custom-call | tf_op jit(solution)/shard_map/exchange/pallas_call | solution.py:344
  27.3 3.8 %update.1 = (f32[64,6144]{1,0:T(8,128)}, f32[64,4096]{1,0:T(8,128)}) custom-call(s32[16]{0:T(128)} %bitcast.15, f32[64,6144]{1,0:T(8,128)} %bitcast.10, bf16[16,64,128]{2,1,0:T(8,128)(2,1)} %get-tuple-element.6.ret_in, f32[64,4096]{1,0:T(8,128)} %get-tuple-element.7.new_id), custom_call_target="tpu_custom_call" | custom-call | tf_op jit(solution)/shard_map/update/pallas_call | solution.py:434

commit v8 on v7

--- a/solution.py
+++ b/solution.py
@@ -11,6 +11,7 @@
 UNROLL = 8
 GROUP = 8
 ROUNDS = 4
+WAVE = 4
 PARTS = 4
 VMEM_BYTES = 58 << 20
 F32 = jnp.float32
@@ -167,9 +168,12 @@
             device_id={"gy": other}, device_id_type=MESH,
         )
 
+    def distance(step):
+        return 1 + lax.rem(step - 1 + peers // 4 - 1, peers - 1)
+
     @pl.loop(1, peers)
     def _(step):
-        peer = lax.rem(me + step, peers)
+        peer = lax.rem(me + distance(step), peers)
         left_copy(peer, me).start()
         weight_copy(peer, me).start()
 
@@ -253,13 +257,6 @@
     right_copy(other).wait_recv()
     unrolled(idents, right_gram)
 
-    @pl.loop(1, peers)
-    def _(step):
-        source = lax.rem(me - step + peers, peers)
-        left_copy(source, source).wait_recv()
-        weight_copy(source, source).wait_recv()
-        forward_copy(source, half).start()
-
     running_sums(0, pairs_for(blocks, peers), slot_gram, (total_gram,))
 
     def finish_slot(s):
@@ -272,21 +269,50 @@
         w_left[s + 1] = rows
         gram[s + 1] = dot_nt(rows, full_left(s))
 
-    @pl.loop(0, peers // GROUP)
+    def source_of(step):
+        return lax.rem(me - distance(step) + peers, peers)
+
+    @pl.loop(0, peers // WAVE + 1)
     def _(i):
-        sources = [lax.rem(me - (i * GROUP + u) + peers, peers) for u in range(GROUP)]
-        for source in sources:
-            forward_copy(source, other).wait_recv()
-        for source in sources:
-            finish_slot(source)
-        for u, source in enumerate(sources):
-            if u > 0:
-                back_copy(source, me).start()
-            else:
-
-                @pl.when(i > 0)
-                def _():
-                    back_copy(source, me).start()
+        def relay(step):
+            source = source_of(step)
+            left_copy(source, source).wait_recv()
+            weight_copy(source, source).wait_recv()
+            forward_copy(source, half).start()
+
+        @pl.when(i < peers // WAVE)
+        def _():
+            for u in range(1, WAVE):
+                relay(i * WAVE + u)
+
+            @pl.when(i > 0)
+            def _():
+                relay(i * WAVE)
+
+        @pl.when(i > 0)
+        def _():
+            first = (i - 1) * WAVE
+            for u in range(1, WAVE):
+                forward_copy(source_of(first + u), other).wait_recv()
+
+            @pl.when(first > 0)
+            def _():
+                forward_copy(source_of(first), other).wait_recv()
+
+            @pl.when(first == 0)
+            def _():
+                forward_copy(me, other).wait_recv()
+                finish_slot(me)
+
+            @pl.when(first > 0)
+            def _():
+                finish_slot(source_of(first))
+                back_copy(source_of(first), me).start()
+
+            for u in range(1, WAVE):
+                finish_slot(source_of(first + u))
+            for u in range(1, WAVE):
+                back_copy(source_of(first + u), me).start()
 
     id_plan = sort_by(1, id_row)
     ret[me] = back[me]
@@ -403,25 +429,30 @@
     load_ret = pltpu.make_async_copy(ret_in, ret, sem.at[0])
     load_id = pltpu.make_async_copy(new_id, ids, sem.at[1])
     store_id = pltpu.make_async_copy(ids, id_out, sem.at[1])
-    for k in range(PARTS):
+    load_ret.start()
+    load(0).start()
+    load_id.start()
+    for k in range(1, PARTS):
         load(k).start()
-    load_ret.start()
-    load_id.start()
     shrink = 1.0 - RATE * DECAY
+    load_ret.wait()
     for k in range(PARTS):
         load(k).wait()
         rec[:, part(k)] = rec[:, part(k)] * shrink
-    load_ret.wait()
-
-    @pl.loop(0, ret.shape[0])
-    def _(s):
-        cols = pl.ds(pl.multiple_of(send_list[s] * blk, blk), blk)
-        rec[:, cols] = rec[:, cols] - RATE * ret[s].astype(F32)
-
-    for k in range(PARTS):
+
+        @pl.loop(0, ret.shape[0])
+        def _(s):
+            block = send_list[s]
+
+            @pl.when(block // (width // blk) == k)
+            def _():
+                cols = pl.ds(pl.multiple_of(block * blk, blk), blk)
+                rec[:, cols] = rec[:, cols] - RATE * ret[s].astype(F32)
+
         store(k).start()
-    load_id.wait()
-    store_id.start()
+        if k == 0:
+            load_id.wait()
+            store_id.start()
     for k in range(PARTS):
         store(k).wait()
     store_id.wait()

time: 31.4 us -> 31.1 us (level)
    pallas_call x1, Pallas kernels: 26.6 us -> 25.8 us  [exchange(): pl.pallas_call(exchange_kernel, out_shape=(jax.ShapeDtypeStruct((peers, h...]
    pallas_call x1, Pallas kernels: 3.85 us -> 4.44 us  [update(): pl.pallas_call(update_kernel, out_shape=(jax.ShapeDtypeStruct(rec_t.shape...]
where the time goes in v8:
time: 31.1 us; the launch traced here: 30.9 us
  Pallas kernels  30.3 us (97%)
  between operations  0.64 us (2%)
    pallas_call x1, Pallas kernels, exchange(): pl.pallas_call(exchange_kernel, out_shape=(jax.ShapeDtypeStruct((peers, h...  25.8 us
    pallas_call x1, Pallas kernels, update(): pl.pallas_call(update_kernel, out_shape=(jax.ShapeDtypeStruct(rec_t.shape...  4.44 us

profile of v8, /device:TPU:0, one launch (start us, length us, event | category | flops | bytes accessed | tf_op | source)
XLA Modules:
  0.0 30.9 jit_solution(16004725855252388712)
XLA Ops:
  0.6 25.8 %exchange.1 = (bf16[16,64,128]{2,1,0:T(8,128)(2,1)}, f32[64,4096]{1,0:T(8,128)}) custom-call(s32[16]{0:T(128)} %bitcast.14, s32[1,192]{1,0:T(1,128)} %bitcast.16, s32[1,192]{1,0:T(1,128)} %bitcast.17, s32[48,128]{1,0:T(8,128)} %bitcast.12, s32[32,128]{1,0:T(8,128)} %bitcast.13, f32[64,6144]{1,0:T(8,128)} %bitcast.9, f32[64,4096]{1,0:T(8,128)} %bitcast.11, ...), custom_call_target="tpu_custom_call" | custom-call | tf_op jit(solution)/shard_map/exchange/pallas_call | solution.py:370
  26.4 4.4 %update.1 = (f32[64,6144]{1,0:T(8,128)}, f32[64,4096]{1,0:T(8,128)}) custom-call(s32[16]{0:T(128)} %bitcast.15, f32[64,6144]{1,0:T(8,128)} %bitcast.10, bf16[16,64,128]{2,1,0:T(8,128)(2,1)} %get-tuple-element.6.ret_in, f32[64,4096]{1,0:T(8,128)} %get-tuple-element.7.new_id), custom_call_target="tpu_custom_call" | custom-call | tf_op jit(solution)/shard_map/update/pallas_call | solution.py:465

commit v9 on v8

--- a/solution.py
+++ b/solution.py
@@ -435,24 +435,22 @@
     for k in range(1, PARTS):
         load(k).start()
     shrink = 1.0 - RATE * DECAY
-    load_ret.wait()
     for k in range(PARTS):
         load(k).wait()
         rec[:, part(k)] = rec[:, part(k)] * shrink
-
-        @pl.loop(0, ret.shape[0])
-        def _(s):
-            block = send_list[s]
-
-            @pl.when(block // (width // blk) == k)
-            def _():
-                cols = pl.ds(pl.multiple_of(block * blk, blk), blk)
-                rec[:, cols] = rec[:, cols] - RATE * ret[s].astype(F32)
-
+    load_id.wait()
+    store_id.start()
+    load_ret.wait()
+
+    @pl.loop(0, ret.shape[0] // GROUP)
+    def _(i):
+        for u in range(GROUP):
+            s = i * GROUP + u
+            cols = pl.ds(pl.multiple_of(send_list[s] * blk, blk), blk)
+            rec[:, cols] = rec[:, cols] - RATE * ret[s].astype(F32)
+
+    for k in range(PARTS):
         store(k).start()
-        if k == 0:
-            load_id.wait()
-            store_id.start()
     for k in range(PARTS):
         store(k).wait()
     store_id.wait()

time: 31.1 us -> 30.7 us (0.987)
  Pallas kernels: 30.3 us -> 29.8 us
    pallas_call x1, Pallas kernels: 4.44 us -> 3.98 us  [update(): pl.pallas_call(update_kernel, out_shape=(jax.ShapeDtypeStruct(rec_t.shape...]
where the time goes in v9:
time: 30.7 us; the launch traced here: 30.4 us
  Pallas kernels  29.8 us (97%)
  between operations  0.64 us (2%)
    pallas_call x1, Pallas kernels, exchange(): pl.pallas_call(exchange_kernel, out_shape=(jax.ShapeDtypeStruct((peers, h...  25.8 us
    pallas_call x1, Pallas kernels, update(): pl.pallas_call(update_kernel, out_shape=(jax.ShapeDtypeStruct(rec_t.shape...  3.98 us

profile of v9, /device:TPU:0, one launch (start us, length us, event | category | flops | bytes accessed | tf_op | source)
XLA Modules:
  0.0 30.4 jit_solution(15779719023757038291)
XLA Ops:
  0.6 25.8 %exchange.1 = (bf16[16,64,128]{2,1,0:T(8,128)(2,1)}, f32[64,4096]{1,0:T(8,128)}) custom-call(s32[16]{0:T(128)} %bitcast.14, s32[1,192]{1,0:T(1,128)} %bitcast.16, s32[1,192]{1,0:T(1,128)} %bitcast.17, s32[48,128]{1,0:T(8,128)} %bitcast.12, s32[32,128]{1,0:T(8,128)} %bitcast.13, f32[64,6144]{1,0:T(8,128)} %bitcast.9, f32[64,4096]{1,0:T(8,128)} %bitcast.11, ...), custom_call_target="tpu_custom_call" | custom-call | tf_op jit(solution)/shard_map/exchange/pallas_call | solution.py:370
  26.4 4.0 %update.1 = (f32[64,6144]{1,0:T(8,128)}, f32[64,4096]{1,0:T(8,128)}) custom-call(s32[16]{0:T(128)} %bitcast.15, f32[64,6144]{1,0:T(8,128)} %bitcast.10, bf16[16,64,128]{2,1,0:T(8,128)(2,1)} %get-tuple-element.6.ret_in, f32[64,4096]{1,0:T(8,128)} %get-tuple-element.7.new_id), custom_call_target="tpu_custom_call" | custom-call | tf_op jit(solution)/shard_map/update/pallas_call | solution.py:463
